TPU v7x, 512 devices: a whole 4x4x16 slice. The times are simulated.
512 devices in a mesh: member: 32 (over z_lo, x, core), band: 16 (over z_hi, y).
Axes of the slice: x: 4, y: 4, z: 16 (z_hi: 4, z_lo: 4; z = z_hi * 4 + z_lo), core: 2. Of those that a mesh axis runs over, the one named last changes fastest.
Arguments:
- controls: float32 [64, 16, 256, 512], P('member', None, 'band'), may hold values from -6 to 6
- members: float32 [64, 16, 256, 512], P('member', None, 'band'), may hold values from -6 to 6
- loc_lon: float32 [512, 512], replicated, may hold values from -0.25 to 0.25
- loc_lat: float32 [256, 256], replicated, may hold values from -0.375 to 0.375
- balance: float32 [5, 1024, 2048], P(None, 'band', 'member'), may hold values from -1 to 1
- innovation: float32 [16, 1024, 2048], P(None, 'band', 'member'), may hold values from -6 to 6
- obs_weight: float32 [16, 1024, 2048], P(None, 'band', 'member'), may hold values from 0.2 to 5
Outputs:
- gradient: float32 [64, 16, 256, 512], P('member', None, 'band')
All inputs are finite; a program needn't handle non-finite values.
Results may differ from a plain program's by a relative error of at most 0.00012.
Values sent between devices are 32-bit elements; how exact they have to be, the bound alone decides.
A program may use at most 64 MiB of HBM per device.

v0:
```python
import math

import jax
import jax.numpy as jnp
from jax import lax
from jax.sharding import Mesh
from jax.sharding import PartitionSpec as P

BAND = ("band_0", "band_1")


phase_fraction = (0.625, 0.875, 0.125, 0.375)
phase_start = (0, 0, 1, 1)


def sent_together(arrays, axis, split_dim, concat_dim, along):
    ends, at = ([], 0)
    for a in arrays[:-1]:
        at += a.shape[along]
        ends.append(at)
    both = jnp.concatenate(arrays, axis=along)
    return tuple(
        jnp.split(
            lax.all_to_all(both, axis, split_axis=split_dim, concat_axis=concat_dim, tiled=True),
            ends,
            axis=along,
        )
    )


def split_up(value, dim, length):
    before, after = (value.shape[:dim], value.shape[dim + 1 :])
    return jnp.moveaxis(value.reshape(*before, length, -1, *after), dim, 0)


def sum_at_owner(value, axis, dim):
    parts = split_up(value, dim, lax.axis_size(axis))
    arrived = lax.all_to_all(parts, axis, split_axis=0, concat_axis=0, tiled=True)
    return arrived.sum(axis=0)


def laid_out(parts, dim):
    shape = list(parts.shape[1:])
    shape[dim] *= parts.shape[0]
    return jnp.moveaxis(parts, 0, dim).reshape(shape)


def turned_blocks(parts, axes, sequence):
    shape = [lax.axis_size(a) for a in axes]
    parts = parts.reshape(*shape, *parts.shape[1:])
    for k in sequence:
        parts = lax.all_to_all(parts, axes[k], split_axis=k, concat_axis=k, tiled=True)
    return parts.reshape(-1, *parts.shape[len(axes) :])


def exchange_by_axis(value, axes, sequence, split_dim, concat_dim):
    parts = split_up(value, split_dim, lax.axis_size(axes))
    return laid_out(turned_blocks(parts, axes, sequence), concat_dim)


def with_halo(value, sides, width, wrap):
    for axis, dim in sides:
        size, length = (lax.axis_size(axis), value.shape[dim])
        up = [(i, (i + 1) % size) for i in range(size if wrap else size - 1)]
        down = [(j, i) for i, j in up]
        last = lax.slice_in_dim(value, length - width, length, axis=dim)
        leading = lax.slice_in_dim(value, 0, width, axis=dim)
        before = lax.ppermute(last, axis, up)
        after = lax.ppermute(leading, axis, down)
        value = jnp.concatenate([before, value, after], axis=dim)
    return value


def copy_for_each(value, axis):
    length = lax.axis_size(axis)
    return lax.all_to_all(
        jnp.broadcast_to(value[None], (length, *value.shape)), axis, 0, 0, tiled=True
    )


def collect(value, axis, dim):
    return laid_out(copy_for_each(value, axis), dim)


def cubic_weights(fraction):
    return (
        (-(fraction**3) + 2 * fraction**2 - fraction) / 2,
        (3 * fraction**3 - 5 * fraction**2 + 2) / 2,
        (-3 * fraction**3 + 4 * fraction**2 + fraction) / 2,
        (fraction**3 - fraction**2) / 2,
    )


def refine(padded, dim_index):
    length = padded.shape[dim_index] - 4
    phase_rows = []
    for phase_index in range(4):
        weights = cubic_weights(phase_fraction[phase_index])
        summed = jnp.zeros_like(lax.slice_in_dim(padded, 0, length, axis=dim_index))
        for tap_index in range(4):
            first = phase_start[phase_index] + tap_index
            summed = summed + weights[tap_index] * lax.slice_in_dim(
                padded, first, first + length, axis=dim_index
            )
        phase_rows.append(summed)
    stacked = jnp.stack(phase_rows, axis=dim_index + 1)
    new_shape = list(padded.shape)
    new_shape[dim_index] = 4 * length
    return stacked.reshape(new_shape)


def refine_both(padded):
    return refine(refine(padded, 1), 2)


def body(controls, members, loc_lon, loc_lat, balance, innovation, obs_weight):
    highest = lax.Precision.HIGHEST
    member_scale = 1.0 / math.sqrt(controls.shape[0] * lax.axis_size("member") - 1)
    level_ctrl, level_members = sent_together((controls, members), BAND, 1, 2, 0)
    rowwise = jnp.einsum("klyx,ux->klyu", level_ctrl, loc_lon, precision=highest)
    fields = jnp.einsum("vy,klyx->klvx", loc_lat, rowwise, precision=highest)
    partial_value = jnp.sum(level_members * fields, axis=0) * member_scale
    share_sum = sum_at_owner(partial_value, "member", 2)
    share_sum = exchange_by_axis(share_sum, BAND, (0, 1), 1, 0)
    extended = with_halo(share_sum, (("member", 2),), 2, True)
    padded = with_halo(extended, ((BAND, 1),), 2, False)
    fine_field = refine_both(padded)
    grown_field = with_halo(fine_field, (("member", 2),), 1, True)
    grown_field = with_halo(grown_field, ((BAND, 1),), 1, False)
    balanced = (
        balance[0] * fine_field
        + balance[1] * grown_field[:, 1:-1, 2:]
        + balance[2] * grown_field[:, 1:-1, :-2]
        + balance[3] * grown_field[:, 2:, 1:-1]
        + balance[4] * grown_field[:, :-2, 1:-1]
    )
    weighted_misfit = obs_weight * (balanced - innovation)
    pieces = balance[1:, None] * weighted_misfit[None]
    spread = with_halo(pieces, (("member", 3),), 1, True)
    spread = with_halo(spread, ((BAND, 2),), 1, False)
    fine_grad = (
        balance[0] * weighted_misfit
        + spread[0][:, 1:-1, :-2]
        + spread[1][:, 1:-1, 2:]
        + spread[2][:, :-2, 1:-1]
        + spread[3][:, 2:, 1:-1]
    )
    fine_halo = with_halo(fine_grad, (("member", 2),), 8, True)
    fine_halo = with_halo(fine_halo, ((BAND, 1),), 8, False)
    template = jnp.zeros((padded.shape[0], padded.shape[1] + 4, padded.shape[2] + 4), jnp.float32)
    unused, pullback = jax.vjp(refine_both, template)
    coarse_grad = pullback(fine_halo)[0][:, 4:-4, 4:-4]
    level_grad = lax.all_to_all(coarse_grad, BAND, split_axis=0, concat_axis=1, tiled=True)
    weighted = level_members * collect(level_grad, "member", 2)[None] * member_scale
    adjoint = jnp.einsum("klyu,ux->klyx", weighted, loc_lon, precision=highest)
    adjoint = jnp.einsum("vy,klvx->klyx", loc_lat, adjoint, precision=highest)
    adjoint = lax.all_to_all(adjoint, BAND, split_axis=2, concat_axis=1, tiled=True)
    return controls + adjoint


def solution(mesh):
    finer = Mesh(mesh.devices.reshape(mesh.shape["member"], 4, 4), ("member", "band_0", "band_1"))
    return jax.shard_map(
        body,
        mesh=finer,
        in_specs=(
            P("member", None, BAND, None),
            P("member", None, BAND, None),
            P(),
            P(),
            P(None, BAND, "member"),
            P(None, BAND, "member"),
            P(None, BAND, "member"),
        ),
        out_specs=P("member", None, BAND, None),
        check_vma=False,
    )
```

profile of v0, /device:TPU:1, one launch (start us, length us, event | category | flops | bytes accessed | tf_op | source)
XLA Modules:
  0.0 417.3 jit_solution(17125132317175494630)
XLA Ops:
  2.2 114.9 %all_to_all.50 = f32[4,16,16,512]{3,2,0,1:T(8,128)S(1)} all-to-all(f32[4,16,16,512]{3,2,0,1:T(8,128)S(1)} %copy.270), channel_id=1, replica_groups=mesh['member'=32,'band_0'=4,'band_1'=4] {'band_0','band_1'}, dimensions={1} | all-to-all | bytes 4194304 | tf_op jit(solution)/shard_map/all_to_all | solution.py:24
  122.0 24.5 %all_to_all.51 = f32[32,1,256,16]{2,3,1,0:T(8,128)S(1)} all-to-all(f32[32,1,256,16]{2,3,1,0:T(8,128)S(1)} %bitcast.262), channel_id=1, replica_groups=mesh['member'=32,'band_0'=4,'band_1'=4] {'member'}, dimensions={0} | all-to-all | bytes 1048576 | tf_op jit(solution)/shard_map/all_to_all | solution.py:38
  146.8 17.8 %all_to_all.52 = f32[4,1,1024]{2,1,0:T(1,128)S(1)} all-to-all(f32[4,1,1024]{2,1,0:T(1,128)S(1)} %reshape.142), channel_id=1, replica_groups=mesh['member'=32,'band_0'=4,'band_1'=4] {'band_0'}, dimensions={0} | all-to-all | bytes 32768 | tf_op jit(solution)/shard_map/all_to_all | solution.py:52
  166.3 6.6 %all_to_all.53 = f32[4,1,1024]{2,1,0:T(1,128)S(1)} all-to-all(f32[4,1,1024]{2,1,0:T(1,128)S(1)} %reshape.144), channel_id=1, replica_groups=mesh['member'=32,'band_0'=4,'band_1'=4] {'band_1'}, dimensions={0} | all-to-all | bytes 32768 | tf_op jit(solution)/shard_map/all_to_all | solution.py:52
  173.9 4.4 %collective-permute-start = (f32[16,16,2]{2,1,0:T(8,128)S(1)}, f32[16,16,2]{2,1,0:T(8,128)S(1)}, u32[]{:S(2)}, u32[]{:S(2)}) collective-permute-start(f32[16,16,2]{2,1,0:T(8,128)S(1)} %get-tuple-element.79), channel_id=1, source_target_pairs={{0,16},{16,32},{32,48},{48,64},{64,80},{80,96},{96,112},{112,128},... | collective-permute-start | bytes 6152 | tf_op jit(solution)/shard_map/ppermute | solution.py:68
  180.3 4.6 %collective-permute-done.1 = f32[16,16,2]{2,1,0:T(8,128)S(1)} collective-permute-done((f32[16,16,2]{2,1,0:T(8,128)S(1)}, f32[16,16,2]{2,1,0:T(8,128)S(1)}, u32[]{:S(2)}, u32[]{:S(2)}) %collective-permute-start.1) | collective-permute-done | bytes 2080 | tf_op jit(solution)/shard_map/ppermute | solution.py:69
  188.6 3.2 collective-permute-done.3
  198.7 2.9 collective-permute-start.5
  201.6 5.7 %collective-permute-start.4 = (f32[16,64,1]{1,0,2:T(8,128)S(1)}, f32[16,64,1]{1,0,2:T(8,128)S(1)}, u32[]{:S(2)}, u32[]{:S(2)}) collective-permute-start(f32[16,64,1]{1,0,2:T(8,128)S(1)} %get-tuple-element.54), channel_id=1, source_target_pairs={{16,0},{32,16},{48,32},{64,48},{80,64},{96,80},{112,96},{128,112},... | collective-permute-start | bytes 12296 | tf_op jit(solution)/shard_map/ppermute | solution.py:69
  209.6 2.7 collective-permute-start.7
  223.5 8.5 %collective-permute-start.9 = (f32[4,16,64,1]{2,1,3,0:T(8,128)S(1)}, f32[4,16,64,1]{2,1,3,0:T(8,128)S(1)}, u32[]{:S(2)}, u32[]{:S(2)}) collective-permute-start(f32[4,16,64,1]{2,1,3,0:T(8,128)S(1)} %get-tuple-element.12), channel_id=1, source_target_pairs={{16,0},{32,16},{48,32},{64,48},{80,64},{96,80},{112,96},{128,112},... | collective-permute-start | bytes 49160 | tf_op jit(solution)/shard_map/ppermute | solution.py:69
  232.9 2.8 fusion.31
  235.7 2.5 copy.238
  238.2 8.9 %collective-permute-start.10 = (f32[4,16,1,66]{3,1,2,0:T(8,128)S(1)}, f32[4,16,1,66]{3,1,2,0:T(8,128)}, u32[]{:S(2)}, u32[]{:S(2)}) collective-permute-start(f32[4,16,1,66]{3,1,2,0:T(8,128)S(1)} %copy.238), channel_id=1, source_target_pairs={{0,1},{1,2},{2,3},{3,4},{4,5},{5,6},{6,7},{7,8},{8,9},{9,10},{10,1... | collective-permute-start | bytes 50696 | tf_op jit(solution)/shard_map/ppermute | solution.py:68
  247.1 3.1 copy.239
  251.5 3.0 copy.240
  255.8 3.0 copy.241
  258.8 3.4 pad_maximum_fusion.1
  265.8 9.4 %collective-permute-start.13 = (f32[16,64,8]{1,0,2:T(8,128)S(1)}, f32[16,64,8]{1,0,2:T(8,128)S(1)}, u32[]{:S(2)}, u32[]{:S(2)}) collective-permute-start(f32[16,64,8]{1,0,2:T(8,128)S(1)} %get-tuple-element.52), channel_id=1, source_target_pairs={{16,0},{32,16},{48,32},{64,48},{80,64},{96,80},{112,96},{128,112},... | collective-permute-start | bytes 98312 | tf_op jit(solution)/shard_map/ppermute | solution.py:69
  276.7 6.8 %collective-permute-start.14 = (f32[16,8,80]{2,1,0:T(8,128)S(1)}, f32[16,8,80]{2,1,0:T(8,128)S(1)}, u32[]{:S(2)}, u32[]{:S(2)}) collective-permute-start(f32[16,8,80]{2,1,0:T(8,128)S(1)} %copy.242), channel_id=1, source_target_pairs={{0,1},{1,2},{2,3},{3,4},{4,5},{5,6},{6,7},{7,8},{8,9},{9,10},{10,1... | collective-permute-start | bytes 122888 | tf_op jit(solution)/shard_map/ppermute | solution.py:68
  285.4 4.5 %collective-permute-done.15 = f32[16,8,80]{2,1,0:T(8,128)S(1)} collective-permute-done((f32[16,8,80]{2,1,0:T(8,128)S(1)}, f32[16,8,80]{2,1,0:T(8,128)S(1)}, u32[]{:S(2)}, u32[]{:S(2)}) %collective-permute-start.15) | collective-permute-done | bytes 40992 | tf_op jit(solution)/shard_map/ppermute | solution.py:69
  292.3 34.5 %all_to_all.54 = f32[16,1,256]{2,1,0:T(1,128)S(1)} all-to-all(f32[16,1,256]{2,1,0:T(1,128)S(1)} %reshape.146), channel_id=1, replica_groups=mesh['member'=32,'band_0'=4,'band_1'=4] {'band_0','band_1'}, dimensions={0} | all-to-all | bytes 32768 | tf_op jit(solution)/shard_map/all_to_all | solution.py:153
  327.7 30.0 %all_to_all.55 = f32[32,1,256,16]{2,3,1,0:T(8,128)S(1)} all-to-all(f32[32,1,256,16]{2,3,1,0:T(8,128)S(1)} %broadcast_in_dim.5), channel_id=1, replica_groups=mesh['member'=32,'band_0'=4,'band_1'=4] {'member'}, dimensions={0} | all-to-all | bytes 1048576 | tf_op jit(solution)/shard_map/all_to_all | solution.py:76
  361.6 54.2 %all_to_all.56 = f32[2,1,256,512]{3,0,1,2:T(2,128)S(1)} all-to-all(f32[2,1,256,512]{3,0,1,2:T(2,128)S(1)} %copy.266), channel_id=1, replica_groups=mesh['member'=32,'band_0'=4,'band_1'=4] {'band_0','band_1'}, dimensions={2} | all-to-all | bytes 2097152 | tf_op jit(solution)/shard_map/all_to_all | solution.py:157
  (133 shorter events, 54.3 us)
Async XLA Ops:
  0.0 119.0 %copy-start = (f32[512,512]{1,0:T(8,128)S(1)}, f32[512,512]{1,0:T(8,128)}, u32[]{:S(2)}) copy-start(f32[512,512]{1,0:T(8,128)} %param.9) | copy-start | bytes 3145732
  117.6 3.2 copy-start.1
  173.9 6.4 %collective-permute-start = (f32[16,16,2]{2,1,0:T(8,128)S(1)}, f32[16,16,2]{2,1,0:T(8,128)S(1)}, u32[]{:S(2)}, u32[]{:S(2)}) collective-permute-start(f32[16,16,2]{2,1,0:T(8,128)S(1)} %get-tuple-element.79), channel_id=1, source_target_pairs={{0,16},{16,32},{32,48},{48,64},{64,80},{80,96},{96,112},{112,128},... | collective-permute-start | bytes 6152 | tf_op jit(solution)/shard_map/ppermute | solution.py:68
  178.4 6.6 %collective-permute-start.1 = (f32[16,16,2]{2,1,0:T(8,128)S(1)}, f32[16,16,2]{2,1,0:T(8,128)S(1)}, u32[]{:S(2)}, u32[]{:S(2)}) collective-permute-start(f32[16,16,2]{2,1,0:T(8,128)S(1)} %get-tuple-element.80), channel_id=1, source_target_pairs={{16,0},{32,16},{48,32},{64,48},{80,64},{96,80},{112,96},{128,112},... | collective-permute-start | bytes 6152 | tf_op jit(solution)/shard_map/ppermute | solution.py:69
  185.1 3.5 collective-permute-start.2
  187.3 4.5 %collective-permute-start.3 = (f32[16,2,20]{2,1,0:T(2,128)S(1)}, f32[16,2,20]{2,1,0:T(2,128)S(1)}, u32[]{:S(2)}, u32[]{:S(2)}) collective-permute-start(f32[16,2,20]{2,1,0:T(2,128)S(1)} %get-tuple-element.78), channel_id=1, source_target_pairs={{1,0},{2,1},{3,2},{4,3},{5,4},{6,5},{7,6},{8,7},{9,8},{10,9},{11,1... | collective-permute-start | bytes 7688 | tf_op jit(solution)/shard_map/ppermute | solution.py:69
  198.7 8.7 %collective-permute-start.5 = (f32[16,64,1]{1,0,2:T(8,128)S(1)}, f32[16,64,1]{1,0,2:T(8,128)S(1)}, u32[]{:S(2)}, u32[]{:S(2)}) collective-permute-start(f32[16,64,1]{1,0,2:T(8,128)S(1)} %get-tuple-element.53), channel_id=1, source_target_pairs={{0,16},{16,32},{32,48},{48,64},{64,80},{80,96},{96,112},{112,128},... | collective-permute-start | bytes 12296 | tf_op jit(solution)/shard_map/ppermute | solution.py:68
  201.6 12.0 %copy-start.8 = (f32[5,64,64]{2,1,0:T(8,128)S(1)}, f32[5,64,64]{2,1,0:T(8,128)}, u32[]{:S(2)}) copy-start(f32[5,64,64]{2,1,0:T(8,128)} %param.11) | copy-start | bytes 245764
  201.6 6.6 %collective-permute-start.4 = (f32[16,64,1]{1,0,2:T(8,128)S(1)}, f32[16,64,1]{1,0,2:T(8,128)S(1)}, u32[]{:S(2)}, u32[]{:S(2)}) collective-permute-start(f32[16,64,1]{1,0,2:T(8,128)S(1)} %get-tuple-element.54), channel_id=1, source_target_pairs={{16,0},{32,16},{48,32},{64,48},{80,64},{96,80},{112,96},{128,112},... | collective-permute-start | bytes 12296 | tf_op jit(solution)/shard_map/ppermute | solution.py:69
  208.2 5.4 %slice-start = ((f32[5,64,64]{2,1,0:T(8,128)}), f32[4,64,64]{2,1,0:T(8,128)S(1)}, s32[]{:S(2)}) async-start(f32[5,64,64]{2,1,0:T(8,128)} %param.11), calls=%async_computation.7 | async-start | bytes 262144 | tf_op jit(solution)/shard_map/slice | solution.py:138
  209.3 8.0 %copy-start.9 = (f32[16,64,64]{2,1,0:T(8,128)S(1)}, f32[16,64,64]{2,1,0:T(8,128)}, u32[]{:S(2)}) copy-start(f32[16,64,64]{2,1,0:T(8,128)} %param.13) | copy-start | bytes 786436
  209.6 9.1 %collective-permute-start.7 = (f32[16,1,66]{2,0,1:T(8,128)S(1)}, f32[16,1,66]{2,0,1:T(8,128)}, u32[]{:S(2)}, u32[]{:S(2)}) collective-permute-start(f32[16,1,66]{2,0,1:T(8,128)S(1)} %copy.233), channel_id=1, source_target_pairs={{0,1},{1,2},{2,3},{3,4},{4,5},{5,6},{6,7},{7,8},{8,9},{9,10},{10,1... | collective-permute-start | bytes 12680 | tf_op jit(solution)/shard_map/ppermute | solution.py:68
  212.3 6.1 %collective-permute-start.6 = (f32[16,1,66]{2,0,1:T(8,128)}, f32[16,1,66]{2,0,1:T(8,128)S(1)}, u32[]{:S(2)}, u32[]{:S(2)}) collective-permute-start(f32[16,1,66]{2,0,1:T(8,128)} %copy.230), channel_id=1, source_target_pairs={{1,0},{2,1},{3,2},{4,3},{5,4},{6,5},{7,6},{8,7},{9,8},{10,9},{11,1... | collective-permute-start | bytes 12680 | tf_op jit(solution)/shard_map/ppermute | solution.py:69
  221.4 10.7 %copy-start.3 = (f32[16,64,64]{1,0,2:T(8,128)}, f32[16,64,64]{1,0,2:T(8,128)S(1)}, u32[]{:S(2)}) copy-start(f32[16,64,64]{1,0,2:T(8,128)S(1)} %fusion.10) | copy-start | bytes 786436
  221.6 10.5 %collective-permute-start.8 = (f32[4,16,64,1]{2,1,3,0:T(8,128)S(1)}, f32[4,16,64,1]{2,1,3,0:T(8,128)S(1)}, u32[]{:S(2)}, u32[]{:S(2)}) collective-permute-start(f32[4,16,64,1]{2,1,3,0:T(8,128)S(1)} %get-tuple-element.11), channel_id=1, source_target_pairs={{0,16},{16,32},{32,48},{48,64},{64,80},{80,96},{96,112},{112,128},... | collective-permute-start | bytes 49160 | tf_op jit(solution)/shard_map/ppermute | solution.py:68
  223.5 9.2 %collective-permute-start.9 = (f32[4,16,64,1]{2,1,3,0:T(8,128)S(1)}, f32[4,16,64,1]{2,1,3,0:T(8,128)S(1)}, u32[]{:S(2)}, u32[]{:S(2)}) collective-permute-start(f32[4,16,64,1]{2,1,3,0:T(8,128)S(1)} %get-tuple-element.12), channel_id=1, source_target_pairs={{16,0},{32,16},{48,32},{64,48},{80,64},{96,80},{112,96},{128,112},... | collective-permute-start | bytes 49160 | tf_op jit(solution)/shard_map/ppermute | solution.py:69
  238.2 13.3 %collective-permute-start.10 = (f32[4,16,1,66]{3,1,2,0:T(8,128)S(1)}, f32[4,16,1,66]{3,1,2,0:T(8,128)}, u32[]{:S(2)}, u32[]{:S(2)}) collective-permute-start(f32[4,16,1,66]{3,1,2,0:T(8,128)S(1)} %copy.238), channel_id=1, source_target_pairs={{0,1},{1,2},{2,3},{3,4},{4,5},{5,6},{6,7},{7,8},{8,9},{9,10},{10,1... | collective-permute-start | bytes 50696 | tf_op jit(solution)/shard_map/ppermute | solution.py:68
  250.2 5.6 %collective-permute-start.11 = (f32[4,16,1,66]{3,1,2,0:T(8,128)}, f32[4,16,1,66]{3,1,2,0:T(8,128)}, u32[]{:S(2)}, u32[]{:S(2)}) collective-permute-start(f32[4,16,1,66]{3,1,2,0:T(8,128)} %copy.239), channel_id=1, source_target_pairs={{1,0},{2,1},{3,2},{4,3},{5,4},{6,5},{7,6},{8,7},{9,8},{10,9},{11,1... | collective-permute-start | bytes 50696 | tf_op jit(solution)/shard_map/ppermute | solution.py:69
  263.8 11.4 %collective-permute-start.12 = (f32[16,64,8]{1,0,2:T(8,128)S(1)}, f32[16,64,8]{1,0,2:T(8,128)S(1)}, u32[]{:S(2)}, u32[]{:S(2)}) collective-permute-start(f32[16,64,8]{1,0,2:T(8,128)S(1)} %get-tuple-element.51), channel_id=1, source_target_pairs={{0,16},{16,32},{32,48},{48,64},{64,80},{80,96},{96,112},{112,128},... | collective-permute-start | bytes 98312 | tf_op jit(solution)/shard_map/ppermute | solution.py:68
  265.8 10.3 %collective-permute-start.13 = (f32[16,64,8]{1,0,2:T(8,128)S(1)}, f32[16,64,8]{1,0,2:T(8,128)S(1)}, u32[]{:S(2)}, u32[]{:S(2)}) collective-permute-start(f32[16,64,8]{1,0,2:T(8,128)S(1)} %get-tuple-element.52), channel_id=1, source_target_pairs={{16,0},{32,16},{48,32},{64,48},{80,64},{96,80},{112,96},{128,112},... | collective-permute-start | bytes 98312 | tf_op jit(solution)/shard_map/ppermute | solution.py:69
  276.7 8.4 %collective-permute-start.14 = (f32[16,8,80]{2,1,0:T(8,128)S(1)}, f32[16,8,80]{2,1,0:T(8,128)S(1)}, u32[]{:S(2)}, u32[]{:S(2)}) collective-permute-start(f32[16,8,80]{2,1,0:T(8,128)S(1)} %copy.242), channel_id=1, source_target_pairs={{0,1},{1,2},{2,3},{3,4},{4,5},{5,6},{6,7},{7,8},{8,9},{9,10},{10,1... | collective-permute-start | bytes 122888 | tf_op jit(solution)/shard_map/ppermute | solution.py:68
  283.7 6.1 %collective-permute-start.15 = (f32[16,8,80]{2,1,0:T(8,128)S(1)}, f32[16,8,80]{2,1,0:T(8,128)S(1)}, u32[]{:S(2)}, u32[]{:S(2)}) collective-permute-start(f32[16,8,80]{2,1,0:T(8,128)S(1)} %copy.243), channel_id=1, source_target_pairs={{1,0},{2,1},{3,2},{4,3},{5,4},{6,5},{7,6},{8,7},{9,8},{10,9},{11,1... | collective-permute-start | bytes 122888 | tf_op jit(solution)/shard_map/ppermute | solution.py:69
  291.8 66.1 %copy-start.2 = (f32[2,16,16,512]{3,2,1,0:T(8,128)S(1)}, f32[2,16,16,512]{3,2,1,0:T(8,128)}, u32[]{:S(2)}) copy-start(f32[2,16,16,512]{3,2,1,0:T(8,128)} %copy-done.1) | copy-start | bytes 3145732
  361.6 54.5 %copy-start.5 = (f32[2,16,16,512]{3,2,1,0:T(8,128)S(1)}, f32[2,16,16,512]{3,2,1,0:T(8,128)}, u32[]{:S(2)}) copy-start(f32[2,16,16,512]{3,2,1,0:T(8,128)} %param.7) | copy-start | bytes 3145732
  (4 other events, 7.8 us)
where the time goes:
time: 421 us; the launch traced here: 417 us
  blocking collectives  282 us (67%)
  starting transfers between devices  62.6 us (15%)
  local copies, waits for them, and re-layouts  35.1 us (8%)
  waiting for transfers between devices  15.9 us (4%)
  other arithmetic  14.6 us (3%)
  matrix products  5.74 us (1%)
    all_to_all x1, blocking collectives, sent_together(): lax.all_to_all(both, axis, split_axis=split_dim, concat_axis=concat_dim,...  115 us
    all_to_all x1, blocking collectives, body(): lax.all_to_all(adjoint, BAND, split_axis=2, concat_axis=1, tiled=True)  54.2 us
    all_to_all x1, blocking collectives, body(): lax.all_to_all(coarse_grad, BAND, split_axis=0, concat_axis=1, tiled=True)  34.5 us
    ppermute x8, starting transfers between devices, with_halo(): before = lax.ppermute(last, axis, up)  31.8 us
    ppermute x8, starting transfers between devices, with_halo(): after = lax.ppermute(leading, axis, down)  30.8 us
    all_to_all x1, blocking collectives, copy_for_each(): lax.all_to_all(jnp.broadcast_to(value[None], (length, *value.shape)), axi...  30 us
    all_to_all x1, blocking collectives, sum_at_owner(): lax.all_to_all(parts, axis, split_axis=0, concat_axis=0, tiled=True)  24.5 us
    all_to_all x2, blocking collectives, turned_blocks(): lax.all_to_all(parts, axes[k], split_axis=k, concat_axis=k, tiled=True)  24.4 us
  transfers between devices with their start and end apart: 16, of which 7 were waited for; matrix products, arithmetic and copies ran while one was open for 3% of the time, Pallas kernels for 0%

commit v1 on v0

v1 whole, which is shorter than its diff:
```python
import math

import jax
import jax.numpy as jnp
import numpy as np
from jax import lax
from jax.experimental import pallas as pl
from jax.experimental.pallas import tpu as pltpu
from jax.sharding import PartitionSpec as P

MESH = pl.DeviceIdType.MESH
BF16 = jnp.bfloat16
F32 = jnp.float32

phase_fraction = (0.625, 0.875, 0.125, 0.375)

KEN, LEVELS, NYC, NXC = 64, 16, 256, 512
BANDS, MEMBERS, XC, ZL = 16, 32, 8, 4
CHUNKS = 2
LC = LEVELS // CHUNKS
LAT, LON = NYC // BANDS, NXC // MEMBERS
SCALE = 1.0 / math.sqrt(KEN - 1)


def cubic_weights(fraction):
    return (
        (-(fraction**3) + 2 * fraction**2 - fraction) / 2,
        (3 * fraction**3 - 5 * fraction**2 + 2) / 2,
        (-3 * fraction**3 + 4 * fraction**2 + fraction) / 2,
        (fraction**3 - fraction**2) / 2,
    )


def refine_rows(shift):
    w = np.zeros((64, 32), np.float32)
    for f in range(64):
        j, r = divmod(f + shift, 4)
        for tap, weight in enumerate(cubic_weights(phase_fraction[r])):
            w[f, j - 2 + tap + (r >= 2) + 8] += weight
    return w


def split_np(w):
    hi = w.astype(BF16)
    lo = (w - hi.astype(np.float32)).astype(BF16)
    return hi, lo


def constants():
    centre, ahead, behind = (refine_rows(s) for s in (0, 1, -1))
    lon = np.zeros((128, 12 * 128), np.float32)
    for s, w in enumerate((centre, ahead, behind)):
        for j in range(4):
            lon[32 * j : 32 * j + 32, (4 * s + j) * 128 : (4 * s + j) * 128 + 64] = w.T
    lh, ll = split_np(lon)
    lon3 = np.concatenate([lh, lh, ll], axis=0)
    th, tl = split_np(np.ascontiguousarray(lon.T))
    lont = np.stack([th, tl])
    lat = np.concatenate([centre, ahead, behind], axis=0)
    ah, al = split_np(lat)
    lat3 = np.concatenate([ah, al, ah], axis=1)
    bh, bl = split_np(np.ascontiguousarray(lat.T))
    latt3 = np.concatenate([bh, bl, bh], axis=1)
    ch, cl = split_np(np.ascontiguousarray(centre.T))
    lattc3 = np.concatenate([ch, cl, ch], axis=1)
    sel = np.zeros((512, 256), np.float32)
    for b in range(BANDS):
        for t in range(32):
            y = 16 * b - 8 + t
            if 0 <= y < NYC:
                sel[32 * b + t, y] = 1
    fold = np.zeros((32, 128), np.float32)
    for j in range(4):
        fold[np.arange(32), 32 * j + np.arange(32)] = 1
    return tuple(
        jnp.asarray(v, BF16)
        for v in (lon3, lont, lat3, latt3, lattc3, sel, np.ascontiguousarray(sel.T), fold)
    )


def split(x):
    hi = x.astype(BF16)
    return hi, (x - hi.astype(F32)).astype(BF16)


def dot(a, b):
    return jnp.dot(a, b, preferred_element_type=F32)


def dot_t(a, b):
    return lax.dot_general(a, b, (((1,), (1,)), ((), ())), preferred_element_type=F32)


def kernel(
    c_ref, m_ref, lonm_ref, latm_ref, bal_ref, inn_ref, ow_ref,
    lon3, lont, lat3, latt3, lattc3, sel, selt, fold,
    out,
    gc, gm, gmt, pt, pa, pbs, pb, sw, z2, r2, ysc, c3, r3, ct, hl, g4, cgt, gb,
    bh, bl, ah, al, bth, btl, ath, atl, bal, inn, ow,
    send, recv, local,
):
    me_m, me_b = lax.axis_index("member"), lax.axis_index("band")
    zl, xc = me_m // XC, me_m % XC

    def band_peer(d):
        return lax.rem(me_b + d, BANDS)

    def on_band(b):
        return {"member": me_m, "band": b}

    def on_member(m):
        return {"member": m, "band": me_b}

    def xc_peer(d):
        return zl * XC + lax.rem(xc + d, XC)

    def zl_peer(d):
        return lax.rem(zl + d, ZL) * XC + xc

    east, west = lax.rem(me_m + 1, MEMBERS), lax.rem(me_m + MEMBERS - 1, MEMBERS)

    barrier = pltpu.get_barrier_semaphore()

    def greet(device):
        pl.semaphore_signal(barrier, inc=1, device_id=device, device_id_type=MESH)

    @pl.loop(1, BANDS)
    def _(d):
        greet(on_band(band_peer(d)))

    @pl.loop(1, XC)
    def _(d):
        greet(on_member(xc_peer(d)))

    @pl.loop(1, ZL)
    def _(d):
        greet(on_member(zl_peer(d)))

    greet(on_member(east))
    greet(on_member(west))
    pl.semaphore_wait(barrier, BANDS - 1 + XC - 1 + ZL - 1 + 2)

    def push(src, dst, ch, ph, device):
        pltpu.make_async_remote_copy(
            src_ref=src, dst_ref=dst, send_sem=send.at[ch, ph], recv_sem=recv.at[ch, ph],
            device_id=device, device_id_type=MESH,
        ).start()

    def wait_for(ref, sem):
        pltpu.make_async_copy(ref, ref, sem).wait()

    def bulk(ch):
        rows = pl.ds(pl.multiple_of(LAT * me_b, LAT), LAT)
        for src, dst, ph in ((c_ref, gc, 0), (m_ref, gm, 1)):

            @pl.loop(1, BANDS)
            def _(d):
                b = band_peer(d)
                push(src.at[lax.rem(b, 2), ch * LC + b // 2], dst.at[ch, rows], ch, ph, on_band(b))

            pltpu.make_async_copy(
                src.at[lax.rem(me_b, 2), ch * LC + me_b // 2], dst.at[ch, rows], local.at[ch, ph]
            ).start()

    def bulk_sent(ch):
        for src, ph in ((gc, 0), (gm, 1)):
            wait_for(src.at[ch, pl.ds(0, 15 * LAT)], send.at[ch, ph])

    def bulk_here(ch, ph):
        src = (gc, gm)[ph]
        wait_for(src.at[ch, pl.ds(0, 15 * LAT)], recv.at[ch, ph])
        wait_for(src.at[ch, pl.ds(0, LAT)], local.at[ch, ph])

    def prepare():
        for ref, hi, lo, thi, tlo in ((lonm_ref, bh, bl, bth, btl), (latm_ref, ah, al, ath, atl)):
            n = ref.shape[0]
            for i in range(n // 128):
                w = ref[pl.ds(128 * i, 128), :]
                h, l = split(w)
                hi[pl.ds(128 * i, 128), :] = h
                lo[pl.ds(128 * i, 128), :] = l
                h, l = split(w.T)
                thi[:, pl.ds(128 * i, 128)] = h
                tlo[:, pl.ds(128 * i, 128)] = l
        for src, dst in ((bal_ref, bal), (inn_ref, inn), (ow_ref, ow)):
            dst[...] = jnp.zeros_like(dst)
            dst[:, :, pl.ds(0, 64)] = src[...]
        row = lax.broadcasted_iota(jnp.int32, (64, 128), 0)
        bal[3] = jnp.where((row == 63) & (me_b == BANDS - 1), 0.0, bal[3])
        bal[4] = jnp.where((row == 0) & (me_b == 0), 0.0, bal[4])

    def fields(ch):
        bulk_here(ch, 0)
        bulk_here(ch, 1)
        for i in range(4):
            gmt[ch, pl.ds(128 * i, 128), :] = gm[ch, :, pl.ds(128 * i, 128)].T
        chh, chl = split(gc[ch])

        @pl.loop(0, 4)
        def _(i):
            rows = pl.ds(pl.multiple_of(128 * i, 128), 128)
            x = dot_t(bh[rows, :], chh) + dot_t(bh[rows, :], chl) + dot_t(bl[rows, :], chh)
            xh, xl = split(x)
            f = dot_t(xh, ah[...]) + dot_t(xl, ah[...]) + dot_t(xh, al[...])
            pt[ch, i] = (f * gmt[ch, rows, :] * SCALE).reshape(XC, LON, NYC)

        @pl.loop(1, XC)
        def _(d):
            p = xc_peer(d)
            push(pt.at[ch, :, lax.rem(p, XC)], pa.at[ch, xc], ch, 2, on_member(p))

        pa[ch, xc] = pt[ch, :, xc]

    def reduce_b(ch):
        wait_for(pa.at[ch, pl.ds(0, XC - 1)], recv.at[ch, 2])
        total = pa[ch, 0]
        for i in range(1, XC):
            total = total + pa[ch, i]
        pbs[ch] = total

        @pl.loop(1, ZL)
        def _(d):
            p = zl_peer(d)
            push(pbs.at[ch, p // XC], pb.at[ch, zl], ch, 3, on_member(p))

        pb[ch, zl] = pbs[ch, zl]

    def halo(ch):
        wait_for(pb.at[ch, pl.ds(0, ZL - 1)], recv.at[ch, 3])
        sw[ch, pl.ds(8, LON)] = pb[ch, 0] + pb[ch, 1] + pb[ch, 2] + pb[ch, 3]
        push(sw.at[ch, pl.ds(8, 8)], sw.at[ch, pl.ds(24, 8)], ch, 4, on_member(west))
        push(sw.at[ch, pl.ds(16, 8)], sw.at[ch, pl.ds(0, 8)], ch, 5, on_member(east))

    def hand_out(ch):
        wait_for(sw.at[ch, pl.ds(24, 8)], recv.at[ch, 4])
        wait_for(sw.at[ch, pl.ds(0, 8)], recv.at[ch, 5])
        w = sw[ch]
        wh, wl = split(jnp.concatenate([w, w, w, w], axis=0))
        z = (dot_t(sel[...], wh) + dot_t(sel[...], wl)).reshape(BANDS, 4, 8, 128)
        group = lax.broadcasted_iota(jnp.int32, (BANDS, 8, 128), 2) // 32
        packed = z[:, 0]
        for j in range(1, 4):
            packed = jnp.where(group == j, z[:, j], packed)
        z2[ch] = packed

        @pl.loop(1, BANDS)
        def _(d):
            b = band_peer(d)
            push(z2.at[ch, b], r2.at[ch, me_b], ch, 6, on_band(b))

        r2[ch, me_b] = z2[ch, me_b]

    def fine(ch):
        wait_for(r2.at[ch, pl.ds(0, BANDS - 1)], recv.at[ch, 6])
        x = r2[ch].reshape(LC, 2, 8, 128)
        xh, xl = split((x[:, 0] + x[:, 1]).reshape(LC * 8, 128))
        y = dot(jnp.concatenate([xh, xl, xh], axis=1), lon3[...])
        for s in range(3):
            for j in range(4):
                for lev in range(LC):
                    ysc[s, pl.ds(8 * j, 8), pl.ds(128 * lev, 128)] = y[
                        8 * lev : 8 * lev + 8, (4 * s + j) * 128 : (4 * s + j + 1) * 128
                    ]

        def stacked(v):
            h, l = split(v)
            return jnp.concatenate([h, h, l], axis=0)

        v_c = dot(lat3[...], stacked(ysc[0]))
        v_e = dot(lat3[pl.ds(0, 64), :], stacked(ysc[1]))
        v_w = dot(lat3[pl.ds(0, 64), :], stacked(ysc[2]))
        to_c, to_e, to_w = [], [], []
        for lev in range(LC):
            at = slice(128 * lev, 128 * lev + 128)
            image = (
                bal[0] * v_c[0:64, at] + bal[1] * v_e[:, at] + bal[2] * v_w[:, at]
                + bal[3] * v_c[64:128, at] + bal[4] * v_c[128:192, at]
            )
            misfit = ow[ch * LC + lev] * (image - inn[ch * LC + lev])
            to_c.append(
                jnp.concatenate([bal[0] * misfit, bal[3] * misfit, bal[4] * misfit], axis=0)
            )
            to_e.append(bal[1] * misfit)
            to_w.append(bal[2] * misfit)
        t = (
            dot(latt3[...], stacked(jnp.concatenate(to_c, axis=1))),
            dot(lattc3[...], stacked(jnp.concatenate(to_e, axis=1))),
            dot(lattc3[...], stacked(jnp.concatenate(to_w, axis=1))),
        )
        rows = []
        for lev in range(LC):
            rows.append(
                jnp.concatenate(
                    [
                        t[s][8 * j : 8 * j + 8, 128 * lev : 128 * lev + 128]
                        for s in range(3)
                        for j in range(4)
                    ],
                    axis=1,
                )
            )
        lh, ll = split(jnp.concatenate(rows, axis=0))
        c3[ch] = (dot(lh, lont[0]) + dot(ll, lont[0]) + dot(lh, lont[1])).reshape(LC, 8, 128)

        @pl.loop(1, BANDS)
        def _(d):
            b = band_peer(d)
            push(c3.at[ch, b // 2], r3.at[ch, me_b], ch, 7, on_band(b))

        r3[ch, me_b] = c3[ch, me_b // 2]

    def gather_in(ch):
        wait_for(r3.at[ch, pl.ds(0, BANDS - 1)], recv.at[ch, 7])
        group = lax.broadcasted_iota(jnp.int32, (BANDS, 8, 128), 2) // 32
        r = r3[ch]
        e = jnp.stack([jnp.where(group == j, r, 0.0) for j in range(4)], axis=1)
        eh, el = split(e.reshape(512, 128))
        oh, ol = split(dot(selt[...], eh) + dot(selt[...], el))
        ct[ch] = dot_t(fold[...], oh) + dot_t(fold[...], ol)
        push(ct.at[ch, pl.ds(0, 8)], hl.at[ch, 1], ch, 8, on_member(west))
        push(ct.at[ch, pl.ds(24, 8)], hl.at[ch, 0], ch, 9, on_member(east))

    def spread_b(ch):
        wait_for(hl.at[ch, 1], recv.at[ch, 8])
        wait_for(hl.at[ch, 0], recv.at[ch, 9])
        own = ct[ch, pl.ds(8, LON)] + jnp.concatenate([hl[ch, 0], hl[ch, 1]], axis=0)
        g4[ch, zl] = own * SCALE

        @pl.loop(1, ZL)
        def _(d):
            push(g4.at[ch, zl], g4.at[ch, zl], ch, 10, on_member(zl_peer(d)))

    def spread_a(ch):
        wait_for(g4.at[ch, pl.ds(0, ZL - 1)], recv.at[ch, 10])

        @pl.loop(1, XC)
        def _(d):
            push(g4.at[ch], cgt.at[ch, :, xc], ch, 11, on_member(xc_peer(d)))

        cgt[ch, :, xc] = g4[ch]

    def adjoint(ch):
        wait_for(cgt.at[ch, :, pl.ds(0, XC - 1)], recv.at[ch, 11])
        wh, wl = split(gmt[ch] * cgt[ch].reshape(NXC, NYC))
        for i in range(4):
            rows = pl.ds(128 * i, 128)
            h = dot(bth[rows, :], wh) + dot(bth[rows, :], wl) + dot(btl[rows, :], wh)
            hh, hlo = split(h)
            gb[ch, :, rows] = dot_t(ath[...], hh) + dot_t(ath[...], hlo) + dot_t(atl[...], hh)
        k, lev = lax.rem(me_b, 2), ch * LC + me_b // 2

        @pl.loop(1, BANDS)
        def _(d):
            b = band_peer(d)
            rows = pl.ds(pl.multiple_of(LAT * b, LAT), LAT)
            push(gb.at[ch, rows], out.at[k, lev], ch, 12, on_band(b))

        out[k, lev] = gb[ch, pl.ds(pl.multiple_of(LAT * me_b, LAT), LAT), :]

    def finish(ch):
        wait_for(gb.at[ch, pl.ds(0, 15 * LAT)], recv.at[ch, 12])
        wait_for(pa.at[ch, pl.ds(0, XC - 1)], send.at[ch, 2])
        wait_for(pb.at[ch, pl.ds(0, ZL - 1)], send.at[ch, 3])
        wait_for(sw.at[ch, pl.ds(0, 8)], send.at[ch, 4])
        wait_for(sw.at[ch, pl.ds(0, 8)], send.at[ch, 5])
        wait_for(r2.at[ch, pl.ds(0, BANDS - 1)], send.at[ch, 6])
        wait_for(r3.at[ch, pl.ds(0, BANDS - 1)], send.at[ch, 7])
        wait_for(hl.at[ch, 1], send.at[ch, 8])
        wait_for(hl.at[ch, 0], send.at[ch, 9])
        wait_for(pb.at[ch, pl.ds(0, ZL - 1)], send.at[ch, 10])
        wait_for(pa.at[ch, pl.ds(0, XC - 1)], send.at[ch, 11])
        wait_for(gb.at[ch, pl.ds(0, 15 * LAT)], send.at[ch, 12])

    bulk(0)
    prepare()
    bulk_sent(0)
    bulk(1)
    for stage in (fields, reduce_b, halo, hand_out, fine, gather_in, spread_b, spread_a, adjoint):
        stage(0)
    for stage in (fields, reduce_b, halo, hand_out, fine, gather_in, spread_b, spread_a, adjoint):
        stage(1)
    bulk_sent(1)
    finish(0)
    finish(1)


def body(controls, members, loc_lon, loc_lat, balance, innovation, obs_weight):
    consts = constants()
    vmem = pl.BlockSpec(memory_space=pltpu.VMEM)
    f32 = lambda *s: pltpu.VMEM(s, F32)
    b16 = lambda *s: pltpu.VMEM(s, BF16)
    adjoint = pl.pallas_call(
        kernel,
        out_shape=jax.ShapeDtypeStruct(controls.shape, F32),
        in_specs=[vmem] * (7 + len(consts)),
        out_specs=vmem,
        scratch_shapes=[
            f32(CHUNKS, NYC, NXC),
            f32(CHUNKS, NYC, NXC),
            f32(CHUNKS, NXC, NYC),
            f32(CHUNKS, ZL, XC, LON, NYC),
            f32(CHUNKS, XC, ZL, LON, NYC),
            f32(CHUNKS, ZL, LON, NYC),
            f32(CHUNKS, ZL, LON, NYC),
            f32(CHUNKS, 32, NYC),
            f32(CHUNKS, BANDS, 8, 128),
            f32(CHUNKS, BANDS, 8, 128),
            f32(3, 32, LC * 128),
            f32(CHUNKS, LC, 8, 128),
            f32(CHUNKS, BANDS, 8, 128),
            f32(CHUNKS, 32, NYC),
            f32(CHUNKS, 2, 8, NYC),
            f32(CHUNKS, ZL, LON, NYC),
            f32(CHUNKS, ZL, XC, LON, NYC),
            f32(CHUNKS, NYC, NXC),
            b16(NXC, NXC), b16(NXC, NXC), b16(NYC, NYC), b16(NYC, NYC),
            b16(NXC, NXC), b16(NXC, NXC), b16(NYC, NYC), b16(NYC, NYC),
            f32(5, 64, 128), f32(LEVELS, 64, 128), f32(LEVELS, 64, 128),
            pltpu.SemaphoreType.DMA((CHUNKS, 13)),
            pltpu.SemaphoreType.DMA((CHUNKS, 13)),
            pltpu.SemaphoreType.DMA((CHUNKS, 2)),
        ],
        compiler_params=pltpu.CompilerParams(
            collective_id=0, has_side_effects=True, vmem_limit_bytes=56 << 20
        ),
        name="gradient",
    )(controls, members, loc_lon, loc_lat, balance, innovation, obs_weight, *consts)
    return controls + adjoint


def solution(mesh):
    return jax.shard_map(
        body,
        mesh=mesh,
        in_specs=(
            P("member", None, "band", None),
            P("member", None, "band", None),
            P(),
            P(),
            P(None, "band", "member"),
            P(None, "band", "member"),
            P(None, "band", "member"),
        ),
        out_specs=P("member", None, "band", None),
        check_vma=False,
    )
```

time: 421 us -> 243 us (0.58)
  blocking collectives: 282 us -> 0 us
  Pallas kernels: 0 us -> 236 us
  starting transfers between devices: 62.6 us -> 0 us
  local copies, waits for them, and re-layouts: 35.1 us -> 0.01 us
  waiting for transfers between devices: 15.9 us -> 0 us
  other arithmetic: 14.6 us -> 2.47 us
  matrix products: 5.74 us -> 0 us
    all_to_all x7 -> x0, blocking collectives: 282 us -> none  [the longest x1 115 us: sent_together(): lax.all_to_all(both, axis, split_axis=split_dim, concat_axis=concat_dim,...]
    pallas_call x0 -> x1, Pallas kernels: none -> 236 us  [body(): pl.pallas_call(kernel, out_shape=jax.ShapeDtypeStruct(controls.shape, F32...]
    ppermute x16 -> x0, starting transfers between devices: 62.6 us -> none  [the longest x8 31.8 us: with_halo(): before = lax.ppermute(last, axis, up)]
    ppermute x16 -> x0, waiting for transfers between devices: 15.9 us -> none  [the longest x8 15.9 us: with_halo(): after = lax.ppermute(leading, axis, down)]
    slice x19 -> x0, local copies, waits for them, and re-layouts: 12.8 us -> none  [the longest x10 6.2 us: with_halo(): last = lax.slice_in_dim(value, length - width, length, axis=dim)]
    ppermute x6 -> x0, local copies, waits for them, and re-layouts: 8.07 us -> none  [the longest x3 4.39 us: with_halo(): before = lax.ppermute(last, axis, up)]
    unnamed x36 -> x2, local copies, waits for them, and re-layouts: 7.69 us -> 0.01 us
    concatenate x8 -> x0, other arithmetic: 6.38 us -> none  [the longest x7 4.5 us: with_halo(): value = jnp.concatenate([before, value, after], axis=dim)]
  transfers between devices with their start and end apart: 16 -> 0, of which waited for: 7 -> 0; matrix products, arithmetic and copies ran while one was open for 3% -> 0% of each run, Pallas kernels for 0% -> 0%
where the time goes in v1:
time: 243 us; the launch traced here: 239 us
  Pallas kernels  236 us (97%)
  other arithmetic  2.47 us (1%)
    pallas_call x1, Pallas kernels, body(): pl.pallas_call(kernel, out_shape=jax.ShapeDtypeStruct(controls.shape, F32...  236 us

profile of v1, /device:TPU:1, one launch (start us, length us, event | category | flops | bytes accessed | tf_op | source)
XLA Modules:
  0.0 238.8 jit_solution(14158607790519598626)
XLA Ops:
  0.0 0.0 copy-start
  0.0 236.3 %gradient.1 = f32[2,16,16,512]{3,2,1,0:T(8,128)} custom-call(f32[2,16,16,512]{3,2,1,0:T(8,128)} %c_ref.1, f32[2,16,16,512]{3,2,1,0:T(8,128)} %m_ref.1, f32[512,512]{1,0:T(8,128)} %lonm_ref.1, f32[256,256]{1,0:T(8,128)} %latm_ref.1, f32[5,64,64]{2,1,0:T(8,128)} %bal_ref.1, f32[16,64,64]{2,1,0:T(8,128)} %inn_ref.1, f32[16,64,64]{2,1,0:T(8,128)} %ow_ref.1, ...), custom_call_target="tpu_custom_call" | custom-call | tf_op jit(solution)/shard_map/gradient/pallas_call | solution.py:392
  236.3 0.0 copy-done
  236.3 2.5 %add.3 = f32[2,16,16,512]{3,2,1,0:T(8,128)} add(f32[2,16,16,512]{3,2,1,0:T(8,128)S(1)} %copy-done, f32[2,16,16,512]{3,2,1,0:T(8,128)} %gradient.1) | non-fusion elementwise | flops 262144 | bytes 3145728 | tf_op jit(solution)/shard_map/add | solution.py:428
Async XLA Ops:
  0.0 236.3 %copy-start = (f32[2,16,16,512]{3,2,1,0:T(8,128)S(1)}, f32[2,16,16,512]{3,2,1,0:T(8,128)}, u32[]{:S(2)}) copy-start(f32[2,16,16,512]{3,2,1,0:T(8,128)} %c_ref.1) | copy-start | bytes 3145732

commit v2 on v1

v2 whole, which is shorter than its diff:
```python
import math

import jax
import jax.numpy as jnp
import numpy as np
from jax import lax
from jax.experimental import pallas as pl
from jax.experimental.pallas import tpu as pltpu
from jax.sharding import PartitionSpec as P

MESH = pl.DeviceIdType.MESH
BF16 = jnp.bfloat16
F32 = jnp.float32

phase_fraction = (0.625, 0.875, 0.125, 0.375)

KEN, LEVELS, NYC, NXC = 64, 16, 256, 512
BANDS, MEMBERS, XC, ZL = 16, 32, 8, 4
ZH, YB = 4, 4
BLOCK = NYC // ZH
LAT, LON = NYC // BANDS, NXC // MEMBERS
SCALE = 1.0 / math.sqrt(KEN - 1)


def cubic_weights(fraction):
    return (
        (-(fraction**3) + 2 * fraction**2 - fraction) / 2,
        (3 * fraction**3 - 5 * fraction**2 + 2) / 2,
        (-3 * fraction**3 + 4 * fraction**2 + fraction) / 2,
        (fraction**3 - fraction**2) / 2,
    )


def refine_rows(shift):
    w = np.zeros((64, 32), np.float32)
    for f in range(64):
        j, r = divmod(f + shift, 4)
        for tap, weight in enumerate(cubic_weights(phase_fraction[r])):
            w[f, j - 2 + tap + (r >= 2) + 8] += weight
    return w


def split_np(w):
    hi = w.astype(BF16)
    lo = (w - hi.astype(np.float32)).astype(BF16)
    return hi, lo


def constants():
    centre, ahead, behind = (refine_rows(s) for s in (0, 1, -1))
    lon = np.zeros((128, 12 * 128), np.float32)
    for s, w in enumerate((centre, ahead, behind)):
        for j in range(4):
            lon[32 * j : 32 * j + 32, (4 * s + j) * 128 : (4 * s + j) * 128 + 64] = w.T
    lh, ll = split_np(lon)
    lon3 = np.concatenate([lh, lh, ll], axis=0)
    th, tl = split_np(np.ascontiguousarray(lon.T))
    lont = np.stack([th, tl])
    lat = np.concatenate([centre, ahead, behind], axis=0)
    ah, al = split_np(lat)
    lat3 = np.concatenate([ah, al, ah], axis=1)
    bh, bl = split_np(np.ascontiguousarray(lat.T))
    latt3 = np.concatenate([bh, bl, bh], axis=1)
    ch, cl = split_np(np.ascontiguousarray(centre.T))
    lattc3 = np.concatenate([ch, cl, ch], axis=1)
    sel = np.zeros((512, 256), np.float32)
    for b in range(BANDS):
        for t in range(32):
            y = 16 * b - 8 + t
            if 0 <= y < NYC:
                sel[32 * b + t, y] = 1
    fold = np.zeros((32, 128), np.float32)
    for j in range(4):
        fold[np.arange(32), 32 * j + np.arange(32)] = 1
    return tuple(
        jnp.asarray(v, BF16)
        for v in (lon3, lont, lat3, latt3, lattc3, sel, np.ascontiguousarray(sel.T), fold)
    )


def split(x):
    hi = x.astype(BF16)
    return hi, (x - hi.astype(F32)).astype(BF16)


def dot(a, b):
    return jnp.dot(a, b, preferred_element_type=F32)


def dot_t(a, b):
    return lax.dot_general(a, b, (((1,), (1,)), ((), ())), preferred_element_type=F32)


def kernel(
    c_hbm, m_hbm, lon_hbm, lat_hbm, bal_hbm, inn_hbm, ow_hbm, *rest
):
    consts_hbm, (
        out,
        lonm, latm, bal_in, inn_in, ow_in,
        lon3, lont, lat3, latt3, lattc3, sel, selt, fold,
        gc, gm, ft, pt, pa, pbs, pb, sw, z2, r2, ysc, c3, r3, ct, hl, g4, cgt, gb, wsc,
        bh, bl, latf, ap3, atph, atpl, bal, inn, ow,
        send, recv, local, loads,
    ) = rest[:8], rest[8:]
    me_m, me_b = lax.axis_index("member"), lax.axis_index("band")
    zl, xc = me_m // XC, me_m % XC
    zh, yb = me_b // YB, me_b % YB
    level = (me_b, lax.rem(me_b + BANDS - YB, BANDS))
    outer = (lax.rem(zh + ZH - 1, ZH), lax.rem(zh + 1, ZH))

    def band_peer(i):
        return lax.rem(me_b + 1 + lax.rem(i + 7, BANDS - 1), BANDS)

    def on_band(b):
        return {"member": me_m, "band": b}

    def on_member(m):
        return {"member": m, "band": me_b}

    def xc_peer(d):
        return zl * XC + lax.rem(xc + d, XC)

    def zl_peer(d):
        return lax.rem(zl + d, ZL) * XC + xc

    east, west = lax.rem(me_m + 1, MEMBERS), lax.rem(me_m + MEMBERS - 1, MEMBERS)

    barrier = pltpu.get_barrier_semaphore()

    def greet(device):
        pl.semaphore_signal(barrier, inc=1, device_id=device, device_id_type=MESH)

    @pl.loop(0, BANDS - 1)
    def _(i):
        greet(on_band(band_peer(i)))

    @pl.loop(1, ZL)
    def _(d):
        greet(on_member(zl_peer(d)))

    @pl.loop(1, XC)
    def _(d):
        greet(on_member(xc_peer(d)))

    greet(on_member(east))
    greet(on_member(west))

    loaded = [
        pltpu.make_async_copy(src, dst, loads.at[n])
        for n, (src, dst) in enumerate(
            zip(
                (lon_hbm, lat_hbm, bal_hbm, inn_hbm, ow_hbm, *consts_hbm),
                (lonm, latm, bal_in, inn_in, ow_in, lon3, lont, lat3, latt3, lattc3, sel, selt, fold),
            )
        )
    ]
    mine = pl.ds(pl.multiple_of(LAT * yb, LAT), LAT)
    mine_all = pl.ds(pl.multiple_of(LAT * me_b, LAT), LAT)
    own = [
        pltpu.make_async_copy(src.at[:, level[s]], dst.at[s, :, rows], local.at[s, n])
        for s in range(2)
        for n, (src, dst, rows) in enumerate(((c_hbm, gc, mine), (m_hbm, gm, mine_all)))
    ]
    for copy in loaded + own:
        copy.start()
    pl.semaphore_wait(barrier, BANDS - 1 + XC - 1 + ZL - 1 + 2)

    def push(src, dst, ph, device):
        pltpu.make_async_remote_copy(
            src_ref=src, dst_ref=dst, send_sem=send.at[ph], recv_sem=recv.at[ph],
            device_id=device, device_id_type=MESH,
        ).start()

    def wait_for(ref, sem):
        pltpu.make_async_copy(ref, ref, sem).wait()

    def level_at(b, slot):
        return b if slot == 0 else lax.rem(b + BANDS - YB, BANDS)

    def send_members(b, slot, ph):
        push(m_hbm.at[:, level_at(b, slot)], gm.at[slot, :, mine_all], ph, on_band(b))

    def send_controls(b, slot, half):
        rows = pl.ds(pl.multiple_of(BLOCK * half + LAT * yb, LAT), LAT)
        push(c_hbm.at[:, level_at(b, slot)], gc.at[slot, :, rows], slot, on_band(b))

    def ahead(y):
        return outer[1] * YB + lax.rem(yb + y, YB)

    def behind(y):
        return outer[0] * YB + lax.rem(yb + y, YB)

    def beside(y):
        return zh * YB + lax.rem(yb + y, YB)

    @pl.loop(0, YB)
    def _(y):
        send_members(ahead(y), 0, 2)
        send_members(behind(y), 1, 3)

    @pl.loop(0, YB)
    def _(y):
        send_controls(ahead(y), 0, 1)
        send_controls(behind(y), 1, 1)

    @pl.loop(1, YB)
    def _(y):
        send_controls(beside(y), 0, 0)
        send_controls(beside(y), 1, 0)

    @pl.loop(0, YB)
    def _(y):
        send_members(behind(y), 0, 4)
        send_members(ahead(y), 1, 5)

    @pl.loop(1, YB)
    def _(y):
        send_members(beside(y), 0, 4)
        send_members(beside(y), 1, 5)

    two = gm.at[0, 0, pl.ds(0, 8 * LAT)]
    seven = gm.at[0, 0, pl.ds(0, 14 * LAT)]

    def block(group):
        return pl.ds(pl.multiple_of(BLOCK * group, BLOCK), BLOCK)

    def relay():
        wait_for(two, recv.at[3])
        rows = block(outer[1])
        push(gm.at[1, :, rows], gm.at[0, :, rows], 6, on_band(outer[0] * YB + yb))
        wait_for(two, recv.at[2])
        rows = block(outer[0])
        push(gm.at[0, :, rows], gm.at[1, :, rows], 7, on_band(outer[1] * YB + yb))

    def prepare():
        for copy in loaded:
            copy.wait()
        for i in range(4):
            rows = pl.ds(128 * i, 128)
            bh[rows, :], bl[rows, :] = split(lonm[rows, :])
        for i in range(2):
            latf[:, pl.ds(128 * i, 128)] = latm[pl.ds(128 * i, 128), :].T
        for s in range(2):
            half = jnp.concatenate([latf[block(zh), :], latf[block(outer[s]), :]], axis=0)
            atph[s], atpl[s] = split(half)
            h, l = split(half.T)
            ap3[s] = jnp.concatenate([h, l, h], axis=1)
        for src, dst in ((bal_in, bal), (inn_in, inn), (ow_in, ow)):
            dst[...] = jnp.zeros_like(dst)
            dst[:, :, pl.ds(0, 64)] = src[...]
        row = lax.broadcasted_iota(jnp.int32, (64, 128), 0)
        bal[3] = jnp.where((row == 63) & (me_b == BANDS - 1), 0.0, bal[3])
        bal[4] = jnp.where((row == 0) & (me_b == 0), 0.0, bal[4])

    def fields():
        for copy in own:
            copy.wait()
        wait_for(seven, recv.at[0])
        wait_for(seven, recv.at[1])

        @pl.loop(0, 2)
        def _(s):
            @pl.loop(0, 2)
            def _(k):
                ch, cl = split(gc[s, k])
                x = dot_t(ch, bh[...]) + dot_t(cl, bh[...]) + dot_t(ch, bl[...])
                xh, xl = split(x)
                ft[s, k] = dot(ap3[s], jnp.concatenate([xh, xh, xl], axis=0))

    def products(s):
        wait_for(seven, recv.at[4 + s])
        wait_for(two, recv.at[6 + s])
        for i in range(ZL):
            at = pl.ds(128 * i, 128)
            p = (gm[s, 0, :, at] * ft[s, 0, :, at] + gm[s, 1, :, at] * ft[s, 1, :, at]) * SCALE
            pt[s, i] = p.T.reshape(XC, LON, NYC)

        @pl.loop(1, XC)
        def _(d):
            p = xc_peer(d)
            push(pt.at[s, :, lax.rem(p, XC)], pa.at[s, xc], 8 + s, on_member(p))

        pa[s, xc] = pt[s, :, xc]

    def reduce_b():
        for s in range(2):
            wait_for(pa.at[s, pl.ds(0, XC - 1)], recv.at[8 + s])
            total = pa[s, 0]
            for i in range(1, XC):
                total = total + pa[s, i]
            pbs[:, s] = total

        @pl.loop(1, ZL)
        def _(d):
            p = zl_peer(d)
            push(pbs.at[p // XC], pb.at[zl], 10, on_member(p))

        pb[zl] = pbs[zl]

    def halo():
        wait_for(pb.at[pl.ds(0, ZL - 1)], recv.at[10])
        sw[:, pl.ds(8, LON)] = pb[0] + pb[1] + pb[2] + pb[3]
        push(sw.at[:, pl.ds(8, 8)], sw.at[:, pl.ds(24, 8)], 11, on_member(west))
        push(sw.at[:, pl.ds(16, 8)], sw.at[:, pl.ds(0, 8)], 12, on_member(east))

    def hand_out():
        wait_for(sw.at[:, pl.ds(24, 8)], recv.at[11])
        wait_for(sw.at[:, pl.ds(0, 8)], recv.at[12])
        w, v = sw[0], sw[1]
        wh, wl = split(jnp.concatenate([w, w, w, w, v, v, v, v], axis=0))
        z = dot_t(sel[...], wh) + dot_t(sel[...], wl)
        group = lax.broadcasted_iota(jnp.int32, (BANDS, 8, 128), 2) // 32
        for s in range(2):
            zs = z[:, 128 * s : 128 * s + 128].reshape(BANDS, 4, 8, 128)
            packed = zs[:, 0]
            for j in range(1, 4):
                packed = jnp.where(group == j, zs[:, j], packed)
            z2[:, s] = packed

        @pl.loop(0, BANDS - 1)
        def _(i):
            b = band_peer(i)
            push(z2.at[b], r2.at[me_b], 13, on_band(b))

        r2[me_b] = z2[me_b]

    def fine():
        wait_for(r2.at[pl.ds(0, BANDS - 1)], recv.at[13])
        x = jnp.concatenate(
            [r2[lev, 0] + r2[(lev + YB) % BANDS, 1] for lev in range(LEVELS)], axis=0
        )
        xh, xl = split(x)
        y = dot(jnp.concatenate([xh, xl, xh], axis=1), lon3[...])
        for s in range(3):
            for j in range(4):
                for lev in range(LEVELS):
                    ysc[s, pl.ds(8 * j, 8), pl.ds(128 * lev, 128)] = y[
                        8 * lev : 8 * lev + 8, (4 * s + j) * 128 : (4 * s + j + 1) * 128
                    ]

        def stacked(v):
            h, l = split(v)
            return jnp.concatenate([h, h, l], axis=0)

        v_c = dot(lat3[...], stacked(ysc[0]))
        v_e = dot(lat3[pl.ds(0, 64), :], stacked(ysc[1]))
        v_w = dot(lat3[pl.ds(0, 64), :], stacked(ysc[2]))
        to_c, to_e, to_w = [], [], []
        for lev in range(LEVELS):
            at = slice(128 * lev, 128 * lev + 128)
            image = (
                bal[0] * v_c[0:64, at] + bal[1] * v_e[:, at] + bal[2] * v_w[:, at]
                + bal[3] * v_c[64:128, at] + bal[4] * v_c[128:192, at]
            )
            misfit = ow[lev] * (image - inn[lev])
            to_c.append(
                jnp.concatenate([bal[0] * misfit, bal[3] * misfit, bal[4] * misfit], axis=0)
            )
            to_e.append(bal[1] * misfit)
            to_w.append(bal[2] * misfit)
        t = (
            dot(latt3[...], stacked(jnp.concatenate(to_c, axis=1))),
            dot(lattc3[...], stacked(jnp.concatenate(to_e, axis=1))),
            dot(lattc3[...], stacked(jnp.concatenate(to_w, axis=1))),
        )
        rows = []
        for lev in range(LEVELS):
            rows.append(
                jnp.concatenate(
                    [
                        t[s][8 * j : 8 * j + 8, 128 * lev : 128 * lev + 128]
                        for s in range(3)
                        for j in range(4)
                    ],
                    axis=1,
                )
            )
        lh, ll = split(jnp.concatenate(rows, axis=0))
        c = dot(lh, lont[0]) + dot(ll, lont[0]) + dot(lh, lont[1])
        for lev in range(LEVELS):
            c3[lev, 0] = c[8 * lev : 8 * lev + 8]
            c3[(lev + YB) % BANDS, 1] = c[8 * lev : 8 * lev + 8]

        @pl.loop(0, BANDS - 1)
        def _(i):
            b = band_peer(i)
            push(c3.at[b], r3.at[me_b], 14, on_band(b))

        r3[me_b] = c3[me_b]

    def gather_in():
        wait_for(r3.at[pl.ds(0, BANDS - 1)], recv.at[14])
        group = lax.broadcasted_iota(jnp.int32, (BANDS, 8, 128), 2) // 32
        both = []
        for s in range(2):
            r = r3[:, s]
            e = jnp.stack([jnp.where(group == j, r, 0.0) for j in range(4)], axis=1)
            both.append(e.reshape(512, 128))
        eh, el = split(jnp.concatenate(both, axis=1))
        oh, ol = split(dot(selt[...], eh) + dot(selt[...], el))
        for s in range(2):
            at = slice(128 * s, 128 * s + 128)
            ct[s] = dot_t(fold[...], oh[:, at]) + dot_t(fold[...], ol[:, at])
        push(ct.at[:, pl.ds(0, 8)], hl.at[1], 15, on_member(west))
        push(ct.at[:, pl.ds(24, 8)], hl.at[0], 16, on_member(east))

    def spread_b():
        wait_for(hl.at[1], recv.at[15])
        wait_for(hl.at[0], recv.at[16])
        own_part = ct[:, pl.ds(8, LON)] + jnp.concatenate([hl[0], hl[1]], axis=1)
        g4[zl] = own_part * SCALE

        @pl.loop(1, ZL)
        def _(d):
            push(g4.at[zl], g4.at[zl], 17, on_member(zl_peer(d)))

    def spread_a():
        wait_for(g4.at[pl.ds(0, ZL - 1)], recv.at[17])
        for s in range(2):

            @pl.loop(1, XC)
            def _(d):
                push(g4.at[:, s], cgt.at[s, :, xc], 18 + s, on_member(xc_peer(d)))

            cgt[s, :, xc] = g4[:, s]

    def adjoint(s):
        wait_for(cgt.at[s, :, pl.ds(0, XC - 1)], recv.at[18 + s])
        for i in range(ZL):
            at = pl.ds(128 * i, 128)
            g = cgt[s, i].reshape(128, NYC).T
            for k in range(2):
                w = gm[s, k, :, at] * g
                h = w.astype(BF16)
                wsc[0, k, :, at] = h
                wsc[1, k, :, at] = (w - h.astype(F32)).astype(BF16)
        for k in range(2):
            t = dot(atph[s], wsc[0, k]) + dot(atpl[s], wsc[0, k]) + dot(atph[s], wsc[1, k])
            th, tl = split(t)
            gb[s, k] = dot(th, bh[...]) + dot(tl, bh[...]) + dot(th, bl[...])

        def give(b, half, y):
            rows = pl.ds(pl.multiple_of(BLOCK * half + LAT * y, LAT), LAT)
            push(gb.at[s, :, rows], out.at[:, level[s]], 20 + s, on_band(b))

        far = (behind, ahead)[s]

        @pl.loop(0, YB)
        def _(y):
            give(far(y), 1, lax.rem(yb + y, YB))

        @pl.loop(1, YB)
        def _(y):
            give(beside(y), 0, lax.rem(yb + y, YB))

        out[:, level[s]] = gb[s, :, mine, :]

    def finish():
        for s in range(2):
            wait_for(seven, recv.at[20 + s])
        for ph in (0, 1, 4, 5, 20, 21):
            wait_for(seven, send.at[ph])
        for ph in (2, 3, 6, 7):
            wait_for(two, send.at[ph])
        for s in range(2):
            wait_for(pa.at[s, pl.ds(0, XC - 1)], send.at[8 + s])
            wait_for(pa.at[s, pl.ds(0, XC - 1)], send.at[18 + s])
        wait_for(pb.at[pl.ds(0, ZL - 1)], send.at[10])
        wait_for(pb.at[pl.ds(0, ZL - 1)], send.at[17])
        wait_for(sw.at[:, pl.ds(24, 8)], send.at[11])
        wait_for(sw.at[:, pl.ds(24, 8)], send.at[12])
        wait_for(r2.at[pl.ds(0, BANDS - 1)], send.at[13])
        wait_for(r3.at[pl.ds(0, BANDS - 1)], send.at[14])
        wait_for(hl.at[1], send.at[15])
        wait_for(hl.at[0], send.at[16])

    relay()
    prepare()
    fields()
    products(0)
    products(1)
    reduce_b()
    halo()
    hand_out()
    fine()
    gather_in()
    spread_b()
    spread_a()
    adjoint(0)
    adjoint(1)
    finish()


def body(controls, members, loc_lon, loc_lat, balance, innovation, obs_weight):
    consts = constants()
    hbm = pl.BlockSpec(memory_space=pl.ANY)
    vmem = pl.BlockSpec(memory_space=pltpu.VMEM)
    f32 = lambda *s: pltpu.VMEM(s, F32)
    b16 = lambda *s: pltpu.VMEM(s, BF16)
    small = (loc_lon, loc_lat, balance, innovation, obs_weight)
    adjoint = pl.pallas_call(
        kernel,
        out_shape=jax.ShapeDtypeStruct(controls.shape, F32),
        in_specs=[hbm] * (7 + len(consts)),
        out_specs=vmem,
        scratch_shapes=[pltpu.VMEM(v.shape, v.dtype) for v in (*small, *consts)]
        + [
            f32(2, 2, 2 * BLOCK, NXC),
            f32(2, 2, NYC, NXC),
            f32(2, 2, NYC, NXC),
            f32(2, ZL, XC, LON, NYC),
            f32(2, XC, ZL, LON, NYC),
            f32(ZL, 2, LON, NYC),
            f32(ZL, 2, LON, NYC),
            f32(2, 32, NYC),
            f32(BANDS, 2, 8, 128),
            f32(BANDS, 2, 8, 128),
            f32(3, 32, LEVELS * 128),
            f32(BANDS, 2, 8, 128),
            f32(BANDS, 2, 8, 128),
            f32(2, 32, NYC),
            f32(2, 2, 8, NYC),
            f32(ZL, 2, LON, NYC),
            f32(2, ZL, XC, LON, NYC),
            f32(2, 2, 2 * BLOCK, NXC),
            b16(2, 2, NYC, NXC),
            b16(NXC, NXC), b16(NXC, NXC), f32(NYC, NYC),
            b16(2, NYC, 6 * BLOCK), b16(2, 2 * BLOCK, NYC), b16(2, 2 * BLOCK, NYC),
            f32(5, 64, 128), f32(LEVELS, 64, 128), f32(LEVELS, 64, 128),
            pltpu.SemaphoreType.DMA((22,)),
            pltpu.SemaphoreType.DMA((22,)),
            pltpu.SemaphoreType.DMA((2, 2)),
            pltpu.SemaphoreType.DMA((13,)),
        ],
        compiler_params=pltpu.CompilerParams(
            collective_id=0, has_side_effects=True, vmem_limit_bytes=56 << 20
        ),
        name="gradient",
    )(controls, members, *small, *consts)
    return controls + adjoint


def solution(mesh):
    return jax.shard_map(
        body,
        mesh=mesh,
        in_specs=(
            P("member", None, "band", None),
            P("member", None, "band", None),
            P(),
            P(),
            P(None, "band", "member"),
            P(None, "band", "member"),
            P(None, "band", "member"),
        ),
        out_specs=P("member", None, "band", None),
        check_vma=False,
    )
```

time: 243 us -> 204 us (0.84)
  Pallas kernels: 236 us -> 199 us
    pallas_call x1, Pallas kernels: 236 us -> 199 us  [body(): pl.pallas_call(kernel, out_shape=jax.ShapeDtypeStruct(controls.shape, F32...]
where the time goes in v2:
time: 204 us; the launch traced here: 201 us
  Pallas kernels  199 us (98%)
  other arithmetic  2.47 us (1%)
    pallas_call x1, Pallas kernels, body(): pl.pallas_call(kernel, out_shape=jax.ShapeDtypeStruct(controls.shape, F32...  199 us

profile of v2, /device:TPU:1, one launch (start us, length us, event | category | flops | bytes accessed | tf_op | source)
XLA Modules:
  0.0 201.0 jit_solution(14314052287734681541)
XLA Ops:
  0.0 0.0 copy-start
  0.0 198.5 %gradient.1 = f32[2,16,16,512]{3,2,1,0:T(8,128)} custom-call(f32[2,16,16,512]{3,2,1,0:T(8,128)} %c_hbm.1, f32[2,16,16,512]{3,2,1,0:T(8,128)} %m_hbm.1, f32[512,512]{1,0:T(8,128)} %lon_hbm.1, f32[256,256]{1,0:T(8,128)} %lat_hbm.1, f32[5,64,64]{2,1,0:T(8,128)} %bal_hbm.1, f32[16,64,64]{2,1,0:T(8,128)} %inn_hbm.1, f32[16,64,64]{2,1,0:T(8,128)} %ow_hbm.1, ...), custom_call_target="tpu_custom_call" | custom-call | tf_op jit(solution)/shard_map/gradient/pallas_call | solution.py:501
  198.5 0.0 copy-done
  198.5 2.5 %add.3 = f32[2,16,16,512]{3,2,1,0:T(8,128)} add(f32[2,16,16,512]{3,2,1,0:T(8,128)S(1)} %copy-done, f32[2,16,16,512]{3,2,1,0:T(8,128)} %gradient.1) | non-fusion elementwise | flops 262144 | bytes 3145728 | tf_op jit(solution)/shard_map/add | solution.py:540
Async XLA Ops:
  0.0 198.5 %copy-start = (f32[2,16,16,512]{3,2,1,0:T(8,128)S(1)}, f32[2,16,16,512]{3,2,1,0:T(8,128)}, u32[]{:S(2)}) copy-start(f32[2,16,16,512]{3,2,1,0:T(8,128)} %c_hbm.1) | copy-start | bytes 3145732

commit v3 on v2

--- a/solution.py
+++ b/solution.py
@@ -51,10 +51,13 @@
     lon = np.zeros((128, 12 * 128), np.float32)
     for s, w in enumerate((centre, ahead, behind)):
         for j in range(4):
-            lon[32 * j : 32 * j + 32, (4 * s + j) * 128 : (4 * s + j) * 128 + 64] = w.T
+            at = (4 * s + j) * 128
+            lon[32 * j : 32 * j + 32, at : at + 64] = w.T
+            lon[32 * j : 32 * j + 32, at + 64 : at + 128] = w.T
     lh, ll = split_np(lon)
     lon3 = np.concatenate([lh, lh, ll], axis=0)
-    th, tl = split_np(np.ascontiguousarray(lon.T))
+    first = (np.arange(12 * 128) % 128 < 64)[:, None]
+    th, tl = split_np(np.concatenate([lon.T * first, lon.T * ~first], axis=1))
     lont = np.stack([th, tl])
     lat = np.concatenate([centre, ahead, behind], axis=0)
     ah, al = split_np(lat)
@@ -98,9 +101,9 @@
         out,
         lonm, latm, bal_in, inn_in, ow_in,
         lon3, lont, lat3, latt3, lattc3, sel, selt, fold,
-        gc, gm, ft, pt, pa, pbs, pb, sw, z2, r2, ysc, c3, r3, ct, hl, g4, cgt, gb, wsc,
+        gc, gm, ft, pt, pa, pbs, pb, pe, sw, z2, r2, ysc, c3, r3, ct, gq, ge, g4, cgt, gb, wsc, ob, cv,
         bh, bl, latf, ap3, atph, atpl, bal, inn, ow,
-        send, recv, local, loads,
+        send, recv, local, loads, ready,
     ) = rest[:8], rest[8:]
     me_m, me_b = lax.axis_index("member"), lax.axis_index("band")
     zl, xc = me_m // XC, me_m % XC
@@ -123,16 +126,39 @@
     def zl_peer(d):
         return lax.rem(zl + d, ZL) * XC + xc
 
-    east, west = lax.rem(me_m + 1, MEMBERS), lax.rem(me_m + MEMBERS - 1, MEMBERS)
-
     barrier = pltpu.get_barrier_semaphore()
 
     def greet(device):
         pl.semaphore_signal(barrier, inc=1, device_id=device, device_id_type=MESH)
 
-    @pl.loop(0, BANDS - 1)
-    def _(i):
-        greet(on_band(band_peer(i)))
+    def ahead(y):
+        return outer[1] * YB + lax.rem(yb + y, YB)
+
+    def behind(y):
+        return outer[0] * YB + lax.rem(yb + y, YB)
+
+    def beside(y):
+        return zh * YB + lax.rem(yb + y, YB)
+
+    def to_east(z):
+        return lax.rem(z * XC + xc + 1, MEMBERS)
+
+    def to_west(z):
+        return lax.rem(z * XC + xc + MEMBERS - 1, MEMBERS)
+
+    @pl.loop(0, YB)
+    def _(y):
+        greet(on_band(ahead(y)))
+        greet(on_band(behind(y)))
+
+    @pl.loop(1, YB)
+    def _(y):
+        greet(on_band(beside(y)))
+
+    @pl.loop(0, ZL)
+    def _(z):
+        greet(on_member(to_east(z)))
+        greet(on_member(to_west(z)))
 
     @pl.loop(1, ZL)
     def _(d):
@@ -141,16 +167,13 @@
     @pl.loop(1, XC)
     def _(d):
         greet(on_member(xc_peer(d)))
-
-    greet(on_member(east))
-    greet(on_member(west))
 
     loaded = [
         pltpu.make_async_copy(src, dst, loads.at[n])
         for n, (src, dst) in enumerate(
             zip(
-                (lon_hbm, lat_hbm, bal_hbm, inn_hbm, ow_hbm, *consts_hbm),
-                (lonm, latm, bal_in, inn_in, ow_in, lon3, lont, lat3, latt3, lattc3, sel, selt, fold),
+                (lon_hbm, lat_hbm, bal_hbm, inn_hbm, ow_hbm, *consts_hbm, c_hbm),
+                (lonm, latm, bal_in, inn_in, ow_in, lon3, lont, lat3, latt3, lattc3, sel, selt, fold, cv),
             )
         )
     ]
@@ -163,7 +186,8 @@
     ]
     for copy in loaded + own:
         copy.start()
-    pl.semaphore_wait(barrier, BANDS - 1 + XC - 1 + ZL - 1 + 2)
+    pl.semaphore_wait(barrier, 3 * YB - 1 + XC - 1 + ZL - 1 + 2 * ZL)
+    pl.semaphore_signal(ready, inc=1, device_id=on_band(behind(0)), device_id_type=MESH)
 
     def push(src, dst, ph, device):
         pltpu.make_async_remote_copy(
@@ -183,15 +207,6 @@
     def send_controls(b, slot, half):
         rows = pl.ds(pl.multiple_of(BLOCK * half + LAT * yb, LAT), LAT)
         push(c_hbm.at[:, level_at(b, slot)], gc.at[slot, :, rows], slot, on_band(b))
-
-    def ahead(y):
-        return outer[1] * YB + lax.rem(yb + y, YB)
-
-    def behind(y):
-        return outer[0] * YB + lax.rem(yb + y, YB)
-
-    def beside(y):
-        return zh * YB + lax.rem(yb + y, YB)
 
     @pl.loop(0, YB)
     def _(y):
@@ -245,9 +260,11 @@
             atph[s], atpl[s] = split(half)
             h, l = split(half.T)
             ap3[s] = jnp.concatenate([h, l, h], axis=1)
-        for src, dst in ((bal_in, bal), (inn_in, inn), (ow_in, ow)):
-            dst[...] = jnp.zeros_like(dst)
-            dst[:, :, pl.ds(0, 64)] = src[...]
+        for n in range(5):
+            bal[n] = jnp.concatenate([bal_in[n], bal_in[n]], axis=1)
+        for p in range(LEVELS // 2):
+            inn[p] = jnp.concatenate([inn_in[2 * p], inn_in[2 * p + 1]], axis=1)
+            ow[p] = jnp.concatenate([ow_in[2 * p], ow_in[2 * p + 1]], axis=1)
         row = lax.broadcasted_iota(jnp.int32, (64, 128), 0)
         bal[3] = jnp.where((row == 63) & (me_b == BANDS - 1), 0.0, bal[3])
         bal[4] = jnp.where((row == 0) & (me_b == 0), 0.0, bal[4])
@@ -290,6 +307,11 @@
                 total = total + pa[s, i]
             pbs[:, s] = total
 
+        @pl.loop(0, ZL)
+        def _(z):
+            push(pbs.at[z, :, pl.ds(8, 8)], pe.at[0, zl], 11, on_member(to_east(z)))
+            push(pbs.at[z, :, pl.ds(0, 8)], pe.at[1, zl], 12, on_member(to_west(z)))
+
         @pl.loop(1, ZL)
         def _(d):
             p = zl_peer(d)
@@ -297,15 +319,13 @@
 
         pb[zl] = pbs[zl]
 
-    def halo():
+    def hand_out():
         wait_for(pb.at[pl.ds(0, ZL - 1)], recv.at[10])
+        wait_for(pe.at[0], recv.at[11])
+        wait_for(pe.at[1], recv.at[12])
         sw[:, pl.ds(8, LON)] = pb[0] + pb[1] + pb[2] + pb[3]
-        push(sw.at[:, pl.ds(8, 8)], sw.at[:, pl.ds(24, 8)], 11, on_member(west))
-        push(sw.at[:, pl.ds(16, 8)], sw.at[:, pl.ds(0, 8)], 12, on_member(east))
-
-    def hand_out():
-        wait_for(sw.at[:, pl.ds(24, 8)], recv.at[11])
-        wait_for(sw.at[:, pl.ds(0, 8)], recv.at[12])
+        sw[:, pl.ds(0, 8)] = pe[0, 0] + pe[0, 1] + pe[0, 2] + pe[0, 3]
+        sw[:, pl.ds(24, 8)] = pe[1, 0] + pe[1, 1] + pe[1, 2] + pe[1, 3]
         w, v = sw[0], sw[1]
         wh, wl = split(jnp.concatenate([w, w, w, w, v, v, v, v], axis=0))
         z = dot_t(sel[...], wh) + dot_t(sel[...], wl)
@@ -316,6 +336,7 @@
             for j in range(1, 4):
                 packed = jnp.where(group == j, zs[:, j], packed)
             z2[:, s] = packed
+        pl.semaphore_wait(ready, 1)
 
         @pl.loop(0, BANDS - 1)
         def _(i):
@@ -327,16 +348,22 @@
     def fine():
         wait_for(r2.at[pl.ds(0, BANDS - 1)], recv.at[13])
         x = jnp.concatenate(
-            [r2[lev, 0] + r2[(lev + YB) % BANDS, 1] for lev in range(LEVELS)], axis=0
+            [
+                r2[lev, 0] + r2[(lev + YB) % BANDS, 1]
+                for first in range(2)
+                for lev in range(first, LEVELS, 2)
+            ],
+            axis=0,
         )
         xh, xl = split(x)
         y = dot(jnp.concatenate([xh, xl, xh], axis=1), lon3[...])
+        left = lax.broadcasted_iota(jnp.int32, (4 * LEVELS, 128), 1) < 64
         for s in range(3):
             for j in range(4):
-                for lev in range(LEVELS):
-                    ysc[s, pl.ds(8 * j, 8), pl.ds(128 * lev, 128)] = y[
-                        8 * lev : 8 * lev + 8, (4 * s + j) * 128 : (4 * s + j + 1) * 128
-                    ]
+                at = slice((4 * s + j) * 128, (4 * s + j + 1) * 128)
+                pair = jnp.where(left, y[: 4 * LEVELS, at], y[4 * LEVELS :, at])
+                for p in range(LEVELS // 2):
+                    ysc[s, pl.ds(8 * j, 8), pl.ds(128 * p, 128)] = pair[8 * p : 8 * p + 8]
 
         def stacked(v):
             h, l = split(v)
@@ -346,13 +373,13 @@
         v_e = dot(lat3[pl.ds(0, 64), :], stacked(ysc[1]))
         v_w = dot(lat3[pl.ds(0, 64), :], stacked(ysc[2]))
         to_c, to_e, to_w = [], [], []
-        for lev in range(LEVELS):
-            at = slice(128 * lev, 128 * lev + 128)
+        for p in range(LEVELS // 2):
+            at = slice(128 * p, 128 * p + 128)
             image = (
                 bal[0] * v_c[0:64, at] + bal[1] * v_e[:, at] + bal[2] * v_w[:, at]
                 + bal[3] * v_c[64:128, at] + bal[4] * v_c[128:192, at]
             )
-            misfit = ow[lev] * (image - inn[lev])
+            misfit = ow[p] * (image - inn[p])
             to_c.append(
                 jnp.concatenate([bal[0] * misfit, bal[3] * misfit, bal[4] * misfit], axis=0)
             )
@@ -364,11 +391,11 @@
             dot(lattc3[...], stacked(jnp.concatenate(to_w, axis=1))),
         )
         rows = []
-        for lev in range(LEVELS):
+        for p in range(LEVELS // 2):
             rows.append(
                 jnp.concatenate(
                     [
-                        t[s][8 * j : 8 * j + 8, 128 * lev : 128 * lev + 128]
+                        t[s][8 * j : 8 * j + 8, 128 * p : 128 * p + 128]
                         for s in range(3)
                         for j in range(4)
                     ],
@@ -378,8 +405,9 @@
         lh, ll = split(jnp.concatenate(rows, axis=0))
         c = dot(lh, lont[0]) + dot(ll, lont[0]) + dot(lh, lont[1])
         for lev in range(LEVELS):
-            c3[lev, 0] = c[8 * lev : 8 * lev + 8]
-            c3[(lev + YB) % BANDS, 1] = c[8 * lev : 8 * lev + 8]
+            p, at = lev // 2, slice(128 * (lev % 2), 128 * (lev % 2) + 128)
+            c3[lev, 0] = c[8 * p : 8 * p + 8, at]
+            c3[(lev + YB) % BANDS, 1] = c[8 * p : 8 * p + 8, at]
 
         @pl.loop(0, BANDS - 1)
         def _(i):
@@ -401,30 +429,36 @@
         for s in range(2):
             at = slice(128 * s, 128 * s + 128)
             ct[s] = dot_t(fold[...], oh[:, at]) + dot_t(fold[...], ol[:, at])
-        push(ct.at[:, pl.ds(0, 8)], hl.at[1], 15, on_member(west))
-        push(ct.at[:, pl.ds(24, 8)], hl.at[0], 16, on_member(east))
-
-    def spread_b():
-        wait_for(hl.at[1], recv.at[15])
-        wait_for(hl.at[0], recv.at[16])
-        own_part = ct[:, pl.ds(8, LON)] + jnp.concatenate([hl[0], hl[1]], axis=1)
-        g4[zl] = own_part * SCALE
+        tile_w = lax.rem(me_m + MEMBERS - 1, MEMBERS) // XC
+        tile_e = lax.rem(me_m + 1, MEMBERS) // XC
+
+        @pl.loop(0, ZL)
+        def _(z):
+            push(ct.at[:, pl.ds(0, 8)], ge.at[1, tile_w], 15, on_member(to_west(z)))
+            push(ct.at[:, pl.ds(24, 8)], ge.at[0, tile_e], 16, on_member(to_east(z)))
 
         @pl.loop(1, ZL)
         def _(d):
-            push(g4.at[zl], g4.at[zl], 17, on_member(zl_peer(d)))
+            push(ct.at[:, pl.ds(8, LON)], gq.at[zl], 17, on_member(zl_peer(d)))
+
+        gq[zl] = ct[:, pl.ds(8, LON)]
 
     def spread_a():
-        wait_for(g4.at[pl.ds(0, ZL - 1)], recv.at[17])
-        for s in range(2):
+        wait_for(gq.at[pl.ds(0, ZL - 1)], recv.at[17])
+        wait_for(ge.at[1], recv.at[15])
+        wait_for(ge.at[0], recv.at[16])
+        for s in range(2):
+            for z in range(ZL):
+                g4[s, z, pl.ds(0, 8)] = (gq[z, s, pl.ds(0, 8)] + ge[0, z, s]) * SCALE
+                g4[s, z, pl.ds(8, 8)] = (gq[z, s, pl.ds(8, 8)] + ge[1, z, s]) * SCALE
 
             @pl.loop(1, XC)
             def _(d):
-                push(g4.at[:, s], cgt.at[s, :, xc], 18 + s, on_member(xc_peer(d)))
-
-            cgt[s, :, xc] = g4[:, s]
-
-    def adjoint(s):
+                push(g4.at[s], cgt.at[s, :, xc], 18 + s, on_member(xc_peer(d)))
+
+            cgt[s, :, xc] = g4[s]
+
+    def weigh(s):
         wait_for(cgt.at[s, :, pl.ds(0, XC - 1)], recv.at[18 + s])
         for i in range(ZL):
             at = pl.ds(128 * i, 128)
@@ -432,32 +466,37 @@
             for k in range(2):
                 w = gm[s, k, :, at] * g
                 h = w.astype(BF16)
-                wsc[0, k, :, at] = h
-                wsc[1, k, :, at] = (w - h.astype(F32)).astype(BF16)
-        for k in range(2):
-            t = dot(atph[s], wsc[0, k]) + dot(atpl[s], wsc[0, k]) + dot(atph[s], wsc[1, k])
-            th, tl = split(t)
-            gb[s, k] = dot(th, bh[...]) + dot(tl, bh[...]) + dot(th, bl[...])
-
-        def give(b, half, y):
-            rows = pl.ds(pl.multiple_of(BLOCK * half + LAT * y, LAT), LAT)
-            push(gb.at[s, :, rows], out.at[:, level[s]], 20 + s, on_band(b))
-
-        far = (behind, ahead)[s]
-
-        @pl.loop(0, YB)
+                wsc[s, 0, k, :, at] = h
+                wsc[s, 1, k, :, at] = (w - h.astype(F32)).astype(BF16)
+
+    def adjoint(s, half):
+        rows = pl.ds(BLOCK * half, BLOCK)
+        ph, plo = atph[s, rows], atpl[s, rows]
+        t = jnp.concatenate(
+            [
+                dot(ph, wsc[s, 0, k]) + dot(plo, wsc[s, 0, k]) + dot(ph, wsc[s, 1, k])
+                for k in range(2)
+            ],
+            axis=0,
+        )
+        th, tl = split(t)
+        g = dot(th, bh[...]) + dot(tl, bh[...]) + dot(th, bl[...])
+        gb[s, 0, rows] = g[:BLOCK]
+        gb[s, 1, rows] = g[BLOCK:]
+        to = (behind, ahead)[s] if half else beside
+
+        @pl.loop(0 if half else 1, YB)
         def _(y):
-            give(far(y), 1, lax.rem(yb + y, YB))
-
-        @pl.loop(1, YB)
-        def _(y):
-            give(beside(y), 0, lax.rem(yb + y, YB))
-
-        out[:, level[s]] = gb[s, :, mine, :]
+            rows = pl.ds(pl.multiple_of(BLOCK * half + LAT * lax.rem(yb + y, YB), LAT), LAT)
+            push(gb.at[s, :, rows], ob.at[:, level[s]], 20 + s, on_band(to(y)))
+
+        if not half:
+            ob[:, level[s]] = gb[s, :, mine, :]
 
     def finish():
         for s in range(2):
             wait_for(seven, recv.at[20 + s])
+        out[...] = ob[...] + cv[...]
         for ph in (0, 1, 4, 5, 20, 21):
             wait_for(seven, send.at[ph])
         for ph in (2, 3, 6, 7):
@@ -467,12 +506,10 @@
             wait_for(pa.at[s, pl.ds(0, XC - 1)], send.at[18 + s])
         wait_for(pb.at[pl.ds(0, ZL - 1)], send.at[10])
         wait_for(pb.at[pl.ds(0, ZL - 1)], send.at[17])
-        wait_for(sw.at[:, pl.ds(24, 8)], send.at[11])
-        wait_for(sw.at[:, pl.ds(24, 8)], send.at[12])
+        for ph in (11, 12, 15, 16):
+            wait_for(pe.at[0], send.at[ph])
         wait_for(r2.at[pl.ds(0, BANDS - 1)], send.at[13])
         wait_for(r3.at[pl.ds(0, BANDS - 1)], send.at[14])
-        wait_for(hl.at[1], send.at[15])
-        wait_for(hl.at[0], send.at[16])
 
     relay()
     prepare()
@@ -480,14 +517,16 @@
     products(0)
     products(1)
     reduce_b()
-    halo()
     hand_out()
     fine()
     gather_in()
-    spread_b()
     spread_a()
-    adjoint(0)
-    adjoint(1)
+    weigh(0)
+    adjoint(0, 1)
+    weigh(1)
+    adjoint(1, 1)
+    adjoint(0, 0)
+    adjoint(1, 0)
     finish()
 
 
@@ -498,7 +537,7 @@
     f32 = lambda *s: pltpu.VMEM(s, F32)
     b16 = lambda *s: pltpu.VMEM(s, BF16)
     small = (loc_lon, loc_lat, balance, innovation, obs_weight)
-    adjoint = pl.pallas_call(
+    return pl.pallas_call(
         kernel,
         out_shape=jax.ShapeDtypeStruct(controls.shape, F32),
         in_specs=[hbm] * (7 + len(consts)),
@@ -512,32 +551,36 @@
             f32(2, XC, ZL, LON, NYC),
             f32(ZL, 2, LON, NYC),
             f32(ZL, 2, LON, NYC),
+            f32(2, ZL, 2, 8, NYC),
             f32(2, 32, NYC),
             f32(BANDS, 2, 8, 128),
             f32(BANDS, 2, 8, 128),
-            f32(3, 32, LEVELS * 128),
+            f32(3, 32, LEVELS * 64),
             f32(BANDS, 2, 8, 128),
             f32(BANDS, 2, 8, 128),
             f32(2, 32, NYC),
-            f32(2, 2, 8, NYC),
             f32(ZL, 2, LON, NYC),
+            f32(2, ZL, 2, 8, NYC),
+            f32(2, ZL, LON, NYC),
             f32(2, ZL, XC, LON, NYC),
             f32(2, 2, 2 * BLOCK, NXC),
-            b16(2, 2, NYC, NXC),
+            b16(2, 2, 2, NYC, NXC),
+            pltpu.VMEM(controls.shape, F32),
+            pltpu.VMEM(controls.shape, F32),
             b16(NXC, NXC), b16(NXC, NXC), f32(NYC, NYC),
             b16(2, NYC, 6 * BLOCK), b16(2, 2 * BLOCK, NYC), b16(2, 2 * BLOCK, NYC),
-            f32(5, 64, 128), f32(LEVELS, 64, 128), f32(LEVELS, 64, 128),
+            f32(5, 64, 128), f32(LEVELS // 2, 64, 128), f32(LEVELS // 2, 64, 128),
             pltpu.SemaphoreType.DMA((22,)),
             pltpu.SemaphoreType.DMA((22,)),
             pltpu.SemaphoreType.DMA((2, 2)),
-            pltpu.SemaphoreType.DMA((13,)),
+            pltpu.SemaphoreType.DMA((14,)),
+            pltpu.SemaphoreType.REGULAR,
         ],
         compiler_params=pltpu.CompilerParams(
             collective_id=0, has_side_effects=True, vmem_limit_bytes=56 << 20
         ),
         name="gradient",
     )(controls, members, *small, *consts)
-    return controls + adjoint
 
 
 def solution(mesh):

time: 204 us -> 201 us (0.985); the launches traced: 201 us -> 201 us
  other arithmetic: 2.47 us -> 0 us
  local copies, waits for them, and re-layouts: 0.01 us -> 2.31 us
    add x1 -> x0, other arithmetic: 2.47 us -> none  [body(): return controls + adjoint]
    unnamed x2 -> x1, local copies, waits for them, and re-layouts: 0.01 us -> 2.31 us
where the time goes in v3:
time: 201 us
  Pallas kernels  198 us (99%)
  local copies, waits for them, and re-layouts  2.31 us (1%)
    pallas_call x1, Pallas kernels, body(): pl.pallas_call(kernel, out_shape=jax.ShapeDtypeStruct(controls.shape, F32...  198 us

profile of v3, /device:TPU:1, one launch (start us, length us, event | category | flops | bytes accessed | tf_op | source)
XLA Modules:
  0.0 200.7 jit_solution(9684506725604185673)
XLA Ops:
  0.0 198.4 %gradient.1 = f32[2,16,16,512]{3,2,1,0:T(8,128)} custom-call(f32[2,16,16,512]{3,2,1,0:T(8,128)} %c_hbm.1, f32[2,16,16,512]{3,2,1,0:T(8,128)} %m_hbm.1, f32[512,512]{1,0:T(8,128)} %lon_hbm.1, f32[256,256]{1,0:T(8,128)} %lat_hbm.1, f32[5,64,64]{2,1,0:T(8,128)} %bal_hbm.1, f32[16,64,64]{2,1,0:T(8,128)} %inn_hbm.1, f32[16,64,64]{2,1,0:T(8,128)} %ow_hbm.1, ...), custom_call_target="tpu_custom_call" | custom-call | tf_op jit(solution)/shard_map/gradient/pallas_call | solution.py:540
  198.4 2.3 %copy.17 = f32[2,16,16,512]{3,2,1,0:T(8,128)} copy(f32[2,16,16,512]{3,2,1,0:T(8,128)} %gradient.1) | data formatting | bytes 2097152

commit v4 on v3

--- a/solution.py
+++ b/solution.py
@@ -101,12 +101,13 @@
         out,
         lonm, latm, bal_in, inn_in, ow_in,
         lon3, lont, lat3, latt3, lattc3, sel, selt, fold,
-        gc, gm, ft, pt, pa, pbs, pb, pe, sw, z2, r2, ysc, c3, r3, ct, gq, ge, g4, cgt, gb, wsc, ob, cv,
+        gc, gm, ft, pt, pc, ps, pa, pbs, pb, sw, z2, r2, ysc, c3, r3, ct, hl, g4, cgt, gb, wsc, ob, cv,
         bh, bl, latf, ap3, atph, atpl, bal, inn, ow,
         send, recv, local, loads, ready,
     ) = rest[:8], rest[8:]
     me_m, me_b = lax.axis_index("member"), lax.axis_index("band")
     zl, xc = me_m // XC, me_m % XC
+    xx, core = xc // 2, xc % 2
     zh, yb = me_b // YB, me_b % YB
     level = (me_b, lax.rem(me_b + BANDS - YB, BANDS))
     outer = (lax.rem(zh + ZH - 1, ZH), lax.rem(zh + 1, ZH))
@@ -120,8 +121,11 @@
     def on_member(m):
         return {"member": m, "band": me_b}
 
-    def xc_peer(d):
-        return zl * XC + lax.rem(xc + d, XC)
+    def x_peer(d):
+        return zl * XC + lax.rem(xx + d, XC // 2) * 2 + core
+
+    other = zl * XC + 2 * xx + 1 - core
+    east, west = lax.rem(me_m + 1, MEMBERS), lax.rem(me_m + MEMBERS - 1, MEMBERS)
 
     def zl_peer(d):
         return lax.rem(zl + d, ZL) * XC + xc
@@ -139,12 +143,6 @@
 
     def beside(y):
         return zh * YB + lax.rem(yb + y, YB)
-
-    def to_east(z):
-        return lax.rem(z * XC + xc + 1, MEMBERS)
-
-    def to_west(z):
-        return lax.rem(z * XC + xc + MEMBERS - 1, MEMBERS)
 
     @pl.loop(0, YB)
     def _(y):
@@ -155,18 +153,17 @@
     def _(y):
         greet(on_band(beside(y)))
 
-    @pl.loop(0, ZL)
-    def _(z):
-        greet(on_member(to_east(z)))
-        greet(on_member(to_west(z)))
+    greet(on_member(east))
+    greet(on_member(west))
+    greet(on_member(other))
 
     @pl.loop(1, ZL)
     def _(d):
         greet(on_member(zl_peer(d)))
 
-    @pl.loop(1, XC)
+    @pl.loop(1, XC // 2)
     def _(d):
-        greet(on_member(xc_peer(d)))
+        greet(on_member(x_peer(d)))
 
     loaded = [
         pltpu.make_async_copy(src, dst, loads.at[n])
@@ -186,7 +183,7 @@
     ]
     for copy in loaded + own:
         copy.start()
-    pl.semaphore_wait(barrier, 3 * YB - 1 + XC - 1 + ZL - 1 + 2 * ZL)
+    pl.semaphore_wait(barrier, 3 * YB - 1 + XC // 2 - 1 + ZL - 1 + 3)
     pl.semaphore_signal(ready, inc=1, device_id=on_band(behind(0)), device_id_type=MESH)
 
     def push(src, dst, ph, device):
@@ -290,27 +287,26 @@
         for i in range(ZL):
             at = pl.ds(128 * i, 128)
             p = (gm[s, 0, :, at] * ft[s, 0, :, at] + gm[s, 1, :, at] * ft[s, 1, :, at]) * SCALE
-            pt[s, i] = p.T.reshape(XC, LON, NYC)
-
-        @pl.loop(1, XC)
+            pt[s, i] = p.T.reshape(XC // 2, 2, LON, NYC)
+
+        push(pt.at[s, :, :, 1 - core], pc.at[s], 22 + s, on_member(other))
+
+    def reduce_a(s):
+        wait_for(pc.at[s], recv.at[22 + s])
+        for z in range(ZL):
+            ps[s, :, z] = pt[s, z, :, core] + pc[s, z]
+
+        @pl.loop(1, XC // 2)
         def _(d):
-            p = xc_peer(d)
-            push(pt.at[s, :, lax.rem(p, XC)], pa.at[s, xc], 8 + s, on_member(p))
-
-        pa[s, xc] = pt[s, :, xc]
+            p = lax.rem(xx + d, XC // 2)
+            push(ps.at[s, p], pa.at[s, xx], 8 + s, on_member(x_peer(d)))
+
+        pa[s, xx] = ps[s, xx]
 
     def reduce_b():
         for s in range(2):
-            wait_for(pa.at[s, pl.ds(0, XC - 1)], recv.at[8 + s])
-            total = pa[s, 0]
-            for i in range(1, XC):
-                total = total + pa[s, i]
-            pbs[:, s] = total
-
-        @pl.loop(0, ZL)
-        def _(z):
-            push(pbs.at[z, :, pl.ds(8, 8)], pe.at[0, zl], 11, on_member(to_east(z)))
-            push(pbs.at[z, :, pl.ds(0, 8)], pe.at[1, zl], 12, on_member(to_west(z)))
+            wait_for(pa.at[s, pl.ds(0, XC // 2 - 1)], recv.at[8 + s])
+            pbs[:, s] = pa[s, 0] + pa[s, 1] + pa[s, 2] + pa[s, 3]
 
         @pl.loop(1, ZL)
         def _(d):
@@ -319,13 +315,15 @@
 
         pb[zl] = pbs[zl]
 
+    def halo():
+        wait_for(pb.at[pl.ds(0, ZL - 1)], recv.at[10])
+        sw[:, pl.ds(8, LON)] = pb[0] + pb[1] + pb[2] + pb[3]
+        push(sw.at[:, pl.ds(8, 8)], sw.at[:, pl.ds(24, 8)], 11, on_member(west))
+        push(sw.at[:, pl.ds(16, 8)], sw.at[:, pl.ds(0, 8)], 12, on_member(east))
+
     def hand_out():
-        wait_for(pb.at[pl.ds(0, ZL - 1)], recv.at[10])
-        wait_for(pe.at[0], recv.at[11])
-        wait_for(pe.at[1], recv.at[12])
-        sw[:, pl.ds(8, LON)] = pb[0] + pb[1] + pb[2] + pb[3]
-        sw[:, pl.ds(0, 8)] = pe[0, 0] + pe[0, 1] + pe[0, 2] + pe[0, 3]
-        sw[:, pl.ds(24, 8)] = pe[1, 0] + pe[1, 1] + pe[1, 2] + pe[1, 3]
+        wait_for(sw.at[:, pl.ds(24, 8)], recv.at[11])
+        wait_for(sw.at[:, pl.ds(0, 8)], recv.at[12])
         w, v = sw[0], sw[1]
         wh, wl = split(jnp.concatenate([w, w, w, w, v, v, v, v], axis=0))
         z = dot_t(sel[...], wh) + dot_t(sel[...], wl)
@@ -429,40 +427,40 @@
         for s in range(2):
             at = slice(128 * s, 128 * s + 128)
             ct[s] = dot_t(fold[...], oh[:, at]) + dot_t(fold[...], ol[:, at])
-        tile_w = lax.rem(me_m + MEMBERS - 1, MEMBERS) // XC
-        tile_e = lax.rem(me_m + 1, MEMBERS) // XC
-
-        @pl.loop(0, ZL)
-        def _(z):
-            push(ct.at[:, pl.ds(0, 8)], ge.at[1, tile_w], 15, on_member(to_west(z)))
-            push(ct.at[:, pl.ds(24, 8)], ge.at[0, tile_e], 16, on_member(to_east(z)))
+        push(ct.at[:, pl.ds(0, 8)], hl.at[1], 15, on_member(west))
+        push(ct.at[:, pl.ds(24, 8)], hl.at[0], 16, on_member(east))
+
+    def spread_b():
+        wait_for(hl.at[1], recv.at[15])
+        wait_for(hl.at[0], recv.at[16])
+        own_part = ct[:, pl.ds(8, LON)] + jnp.concatenate([hl[0], hl[1]], axis=1)
+        g4[zl] = own_part * SCALE
 
         @pl.loop(1, ZL)
         def _(d):
-            push(ct.at[:, pl.ds(8, LON)], gq.at[zl], 17, on_member(zl_peer(d)))
-
-        gq[zl] = ct[:, pl.ds(8, LON)]
+            push(g4.at[zl], g4.at[zl], 17, on_member(zl_peer(d)))
 
     def spread_a():
-        wait_for(gq.at[pl.ds(0, ZL - 1)], recv.at[17])
-        wait_for(ge.at[1], recv.at[15])
-        wait_for(ge.at[0], recv.at[16])
-        for s in range(2):
-            for z in range(ZL):
-                g4[s, z, pl.ds(0, 8)] = (gq[z, s, pl.ds(0, 8)] + ge[0, z, s]) * SCALE
-                g4[s, z, pl.ds(8, 8)] = (gq[z, s, pl.ds(8, 8)] + ge[1, z, s]) * SCALE
-
-            @pl.loop(1, XC)
+        wait_for(g4.at[pl.ds(0, ZL - 1)], recv.at[17])
+        for s in range(2):
+
+            @pl.loop(1, XC // 2)
             def _(d):
-                push(g4.at[s], cgt.at[s, :, xc], 18 + s, on_member(xc_peer(d)))
-
-            cgt[s, :, xc] = g4[s]
+                push(g4.at[:, s], cgt.at[s, core, xx], 18 + s, on_member(x_peer(d)))
+
+            cgt[s, core, xx] = g4[:, s]
+
+    def spread_core(s):
+        wait_for(cgt.at[s, 0, pl.ds(0, XC // 2 - 1)], recv.at[18 + s])
+        push(cgt.at[s, core], cgt.at[s, core], 24 + s, on_member(other))
 
     def weigh(s):
-        wait_for(cgt.at[s, :, pl.ds(0, XC - 1)], recv.at[18 + s])
+        wait_for(cgt.at[s, 0], recv.at[24 + s])
         for i in range(ZL):
             at = pl.ds(128 * i, 128)
-            g = cgt[s, i].reshape(128, NYC).T
+            g = jnp.concatenate(
+                [cgt[s, c, x, i] for x in range(XC // 2) for c in range(2)], axis=0
+            ).T
             for k in range(2):
                 w = gm[s, k, :, at] * g
                 h = w.astype(BF16)
@@ -502,12 +500,14 @@
         for ph in (2, 3, 6, 7):
             wait_for(two, send.at[ph])
         for s in range(2):
-            wait_for(pa.at[s, pl.ds(0, XC - 1)], send.at[8 + s])
-            wait_for(pa.at[s, pl.ds(0, XC - 1)], send.at[18 + s])
+            wait_for(pc.at[s], send.at[22 + s])
+            wait_for(pc.at[s], send.at[24 + s])
+            wait_for(pa.at[s, pl.ds(0, XC // 2 - 1)], send.at[8 + s])
+            wait_for(pa.at[s, pl.ds(0, XC // 2 - 1)], send.at[18 + s])
         wait_for(pb.at[pl.ds(0, ZL - 1)], send.at[10])
         wait_for(pb.at[pl.ds(0, ZL - 1)], send.at[17])
         for ph in (11, 12, 15, 16):
-            wait_for(pe.at[0], send.at[ph])
+            wait_for(hl.at[0], send.at[ph])
         wait_for(r2.at[pl.ds(0, BANDS - 1)], send.at[13])
         wait_for(r3.at[pl.ds(0, BANDS - 1)], send.at[14])
 
@@ -516,11 +516,17 @@
     fields()
     products(0)
     products(1)
+    reduce_a(0)
+    reduce_a(1)
     reduce_b()
+    halo()
     hand_out()
     fine()
     gather_in()
+    spread_b()
     spread_a()
+    spread_core(0)
+    spread_core(1)
     weigh(0)
     adjoint(0, 1)
     weigh(1)
@@ -547,11 +553,12 @@
             f32(2, 2, 2 * BLOCK, NXC),
             f32(2, 2, NYC, NXC),
             f32(2, 2, NYC, NXC),
-            f32(2, ZL, XC, LON, NYC),
-            f32(2, XC, ZL, LON, NYC),
+            f32(2, ZL, XC // 2, 2, LON, NYC),
+            f32(2, ZL, XC // 2, LON, NYC),
+            f32(2, XC // 2, ZL, LON, NYC),
+            f32(2, XC // 2, ZL, LON, NYC),
             f32(ZL, 2, LON, NYC),
             f32(ZL, 2, LON, NYC),
-            f32(2, ZL, 2, 8, NYC),
             f32(2, 32, NYC),
             f32(BANDS, 2, 8, 128),
             f32(BANDS, 2, 8, 128),
@@ -559,10 +566,9 @@
             f32(BANDS, 2, 8, 128),
             f32(BANDS, 2, 8, 128),
             f32(2, 32, NYC),
+            f32(2, 2, 8, NYC),
             f32(ZL, 2, LON, NYC),
-            f32(2, ZL, 2, 8, NYC),
-            f32(2, ZL, LON, NYC),
-            f32(2, ZL, XC, LON, NYC),
+            f32(2, 2, XC // 2, ZL, LON, NYC),
             f32(2, 2, 2 * BLOCK, NXC),
             b16(2, 2, 2, NYC, NXC),
             pltpu.VMEM(controls.shape, F32),
@@ -570,8 +576,8 @@
             b16(NXC, NXC), b16(NXC, NXC), f32(NYC, NYC),
             b16(2, NYC, 6 * BLOCK), b16(2, 2 * BLOCK, NYC), b16(2, 2 * BLOCK, NYC),
             f32(5, 64, 128), f32(LEVELS // 2, 64, 128), f32(LEVELS // 2, 64, 128),
-            pltpu.SemaphoreType.DMA((22,)),
-            pltpu.SemaphoreType.DMA((22,)),
+            pltpu.SemaphoreType.DMA((26,)),
+            pltpu.SemaphoreType.DMA((26,)),
             pltpu.SemaphoreType.DMA((2, 2)),
             pltpu.SemaphoreType.DMA((14,)),
             pltpu.SemaphoreType.REGULAR,

time: 201 us -> 194 us (0.965)
  the two profiles are of different devices: /device:TPU:1 before, /device:TPU:108 now
where the time goes in v4:
time: 194 us
  Pallas kernels  192 us (99%)
  local copies, waits for them, and re-layouts  2.31 us (1%)
    pallas_call x1, Pallas kernels, body(): pl.pallas_call(kernel, out_shape=jax.ShapeDtypeStruct(controls.shape, F32...  192 us

profile of v4, /device:TPU:108, one launch (start us, length us, event | category | flops | bytes accessed | tf_op | source)
XLA Modules:
  0.0 193.9 jit_solution(12227765133320571997)
XLA Ops:
  0.0 191.6 %gradient.1 = f32[2,16,16,512]{3,2,1,0:T(8,128)} custom-call(f32[2,16,16,512]{3,2,1,0:T(8,128)} %c_hbm.1, f32[2,16,16,512]{3,2,1,0:T(8,128)} %m_hbm.1, f32[512,512]{1,0:T(8,128)} %lon_hbm.1, f32[256,256]{1,0:T(8,128)} %lat_hbm.1, f32[5,64,64]{2,1,0:T(8,128)} %bal_hbm.1, f32[16,64,64]{2,1,0:T(8,128)} %inn_hbm.1, f32[16,64,64]{2,1,0:T(8,128)} %ow_hbm.1, ...), custom_call_target="tpu_custom_call" | custom-call | tf_op jit(solution)/shard_map/gradient/pallas_call | solution.py:546
  191.6 2.3 %copy.17 = f32[2,16,16,512]{3,2,1,0:T(8,128)} copy(f32[2,16,16,512]{3,2,1,0:T(8,128)} %gradient.1) | data formatting | bytes 2097152

commit v5 on v4

--- a/solution.py
+++ b/solution.py
@@ -467,29 +467,23 @@
                 wsc[s, 0, k, :, at] = h
                 wsc[s, 1, k, :, at] = (w - h.astype(F32)).astype(BF16)
 
-    def adjoint(s, half):
+    def adjoint(s, half, k):
         rows = pl.ds(BLOCK * half, BLOCK)
         ph, plo = atph[s, rows], atpl[s, rows]
-        t = jnp.concatenate(
-            [
-                dot(ph, wsc[s, 0, k]) + dot(plo, wsc[s, 0, k]) + dot(ph, wsc[s, 1, k])
-                for k in range(2)
-            ],
-            axis=0,
-        )
+        t = dot(ph, wsc[s, 0, k]) + dot(plo, wsc[s, 0, k]) + dot(ph, wsc[s, 1, k])
         th, tl = split(t)
-        g = dot(th, bh[...]) + dot(tl, bh[...]) + dot(th, bl[...])
-        gb[s, 0, rows] = g[:BLOCK]
-        gb[s, 1, rows] = g[BLOCK:]
+        gb[s, k, rows] = dot(th, bh[...]) + dot(tl, bh[...]) + dot(th, bl[...])
+
+    def give(s, half, k):
         to = (behind, ahead)[s] if half else beside
 
         @pl.loop(0 if half else 1, YB)
         def _(y):
             rows = pl.ds(pl.multiple_of(BLOCK * half + LAT * lax.rem(yb + y, YB), LAT), LAT)
-            push(gb.at[s, :, rows], ob.at[:, level[s]], 20 + s, on_band(to(y)))
+            push(gb.at[s, k, rows], ob.at[k, level[s]], 20 + s, on_band(to(y)))
 
         if not half:
-            ob[:, level[s]] = gb[s, :, mine, :]
+            ob[k, level[s]] = gb[s, k, mine, :]
 
     def finish():
         for s in range(2):
@@ -528,11 +522,12 @@
     spread_core(0)
     spread_core(1)
     weigh(0)
-    adjoint(0, 1)
+    adjoint(0, 1, 0)
+    give(0, 1, 0)
     weigh(1)
-    adjoint(1, 1)
-    adjoint(0, 0)
-    adjoint(1, 0)
+    for s, half, k in ((1, 1, 0), (0, 1, 1), (1, 1, 1), (0, 0, 0), (1, 0, 0), (0, 0, 1), (1, 0, 1)):
+        adjoint(s, half, k)
+        give(s, half, k)
     finish()
 
 

time: 194 us -> 192 us (0.990)
  the two profiles are of different devices: /device:TPU:108 before, /device:TPU:96 now
where the time goes in v5:
time: 192 us
  Pallas kernels  190 us (99%)
  local copies, waits for them, and re-layouts  2.31 us (1%)
    pallas_call x1, Pallas kernels, body(): pl.pallas_call(kernel, out_shape=jax.ShapeDtypeStruct(controls.shape, F32...  190 us

profile of v5, /device:TPU:96, one launch (start us, length us, event | category | flops | bytes accessed | tf_op | source)
XLA Modules:
  0.0 192.4 jit_solution(17647324610213025775)
XLA Ops:
  0.0 190.0 %gradient.1 = f32[2,16,16,512]{3,2,1,0:T(8,128)} custom-call(f32[2,16,16,512]{3,2,1,0:T(8,128)} %c_hbm.1, f32[2,16,16,512]{3,2,1,0:T(8,128)} %m_hbm.1, f32[512,512]{1,0:T(8,128)} %lon_hbm.1, f32[256,256]{1,0:T(8,128)} %lat_hbm.1, f32[5,64,64]{2,1,0:T(8,128)} %bal_hbm.1, f32[16,64,64]{2,1,0:T(8,128)} %inn_hbm.1, f32[16,64,64]{2,1,0:T(8,128)} %ow_hbm.1, ...), custom_call_target="tpu_custom_call" | custom-call | tf_op jit(solution)/shard_map/gradient/pallas_call | solution.py:541
  190.0 2.3 %copy.17 = f32[2,16,16,512]{3,2,1,0:T(8,128)} copy(f32[2,16,16,512]{3,2,1,0:T(8,128)} %gradient.1) | data formatting | bytes 2097152

commit v6 on v5

--- a/solution.py
+++ b/solution.py
@@ -210,10 +210,14 @@
         send_members(ahead(y), 0, 2)
         send_members(behind(y), 1, 3)
 
+    def send_far_controls(b, k, ph):
+        rows = pl.ds(pl.multiple_of(BLOCK + LAT * yb, LAT), LAT)
+        push(c_hbm.at[k, level_at(b, 1)], gc.at[1, k, rows], ph, on_band(b))
+
     @pl.loop(0, YB)
     def _(y):
         send_controls(ahead(y), 0, 1)
-        send_controls(behind(y), 1, 1)
+        send_far_controls(behind(y), 0, 1)
 
     @pl.loop(1, YB)
     def _(y):
@@ -232,6 +236,8 @@
 
     two = gm.at[0, 0, pl.ds(0, 8 * LAT)]
     seven = gm.at[0, 0, pl.ds(0, 14 * LAT)]
+    five = gm.at[0, 0, pl.ds(0, 10 * LAT)]
+    four = gm.at[0, 0, pl.ds(0, 4 * LAT)]
 
     def block(group):
         return pl.ds(pl.multiple_of(BLOCK * group, BLOCK), BLOCK)
@@ -240,6 +246,11 @@
         wait_for(two, recv.at[3])
         rows = block(outer[1])
         push(gm.at[1, :, rows], gm.at[0, :, rows], 6, on_band(outer[0] * YB + yb))
+
+        @pl.loop(0, YB)
+        def _(y):
+            send_far_controls(behind(y), 1, 26)
+
         wait_for(two, recv.at[2])
         rows = block(outer[0])
         push(gm.at[0, :, rows], gm.at[1, :, rows], 7, on_band(outer[1] * YB + yb))
@@ -266,20 +277,24 @@
         bal[3] = jnp.where((row == 63) & (me_b == BANDS - 1), 0.0, bal[3])
         bal[4] = jnp.where((row == 0) & (me_b == 0), 0.0, bal[4])
 
+    def field(s, k):
+        ch, cl = split(gc[s, k])
+        x = dot_t(ch, bh[...]) + dot_t(cl, bh[...]) + dot_t(ch, bl[...])
+        xh, xl = split(x)
+        ft[s, k] = dot(ap3[s], jnp.concatenate([xh, xh, xl], axis=0))
+
     def fields():
         for copy in own:
             copy.wait()
         wait_for(seven, recv.at[0])
-        wait_for(seven, recv.at[1])
-
-        @pl.loop(0, 2)
-        def _(s):
-            @pl.loop(0, 2)
-            def _(k):
-                ch, cl = split(gc[s, k])
-                x = dot_t(ch, bh[...]) + dot_t(cl, bh[...]) + dot_t(ch, bl[...])
-                xh, xl = split(x)
-                ft[s, k] = dot(ap3[s], jnp.concatenate([xh, xh, xl], axis=0))
+        wait_for(five, recv.at[1])
+        field(0, 0)
+        field(0, 1)
+        field(1, 0)
+
+    def last_field():
+        wait_for(four, recv.at[26])
+        field(1, 1)
 
     def products(s):
         wait_for(seven, recv.at[4 + s])
@@ -489,8 +504,10 @@
         for s in range(2):
             wait_for(seven, recv.at[20 + s])
         out[...] = ob[...] + cv[...]
-        for ph in (0, 1, 4, 5, 20, 21):
+        for ph in (0, 4, 5, 20, 21):
             wait_for(seven, send.at[ph])
+        wait_for(five, send.at[1])
+        wait_for(four, send.at[26])
         for ph in (2, 3, 6, 7):
             wait_for(two, send.at[ph])
         for s in range(2):
@@ -509,8 +526,9 @@
     prepare()
     fields()
     products(0)
+    reduce_a(0)
+    last_field()
     products(1)
-    reduce_a(0)
     reduce_a(1)
     reduce_b()
     halo()
@@ -571,8 +589,8 @@
             b16(NXC, NXC), b16(NXC, NXC), f32(NYC, NYC),
             b16(2, NYC, 6 * BLOCK), b16(2, 2 * BLOCK, NYC), b16(2, 2 * BLOCK, NYC),
             f32(5, 64, 128), f32(LEVELS // 2, 64, 128), f32(LEVELS // 2, 64, 128),
-            pltpu.SemaphoreType.DMA((26,)),
-            pltpu.SemaphoreType.DMA((26,)),
+            pltpu.SemaphoreType.DMA((27,)),
+            pltpu.SemaphoreType.DMA((27,)),
             pltpu.SemaphoreType.DMA((2, 2)),
             pltpu.SemaphoreType.DMA((14,)),
             pltpu.SemaphoreType.REGULAR,

time: 192 us -> 194 us (1.010)
  the two profiles are of different devices: /device:TPU:96 before, /device:TPU:1 now
where the time goes in v6:
time: 194 us
  Pallas kernels  191 us (98%)
  local copies, waits for them, and re-layouts  2.31 us (1%)
    pallas_call x1, Pallas kernels, body(): pl.pallas_call(kernel, out_shape=jax.ShapeDtypeStruct(controls.shape, F32...  191 us

profile of v6, /device:TPU:1, one launch (start us, length us, event | category | flops | bytes accessed | tf_op | source)
XLA Modules:
  0.0 193.8 jit_solution(723186365277711463)
XLA Ops:
  0.0 191.4 %gradient.1 = f32[2,16,16,512]{3,2,1,0:T(8,128)} custom-call(f32[2,16,16,512]{3,2,1,0:T(8,128)} %c_hbm.1, f32[2,16,16,512]{3,2,1,0:T(8,128)} %m_hbm.1, f32[512,512]{1,0:T(8,128)} %lon_hbm.1, f32[256,256]{1,0:T(8,128)} %lat_hbm.1, f32[5,64,64]{2,1,0:T(8,128)} %bal_hbm.1, f32[16,64,64]{2,1,0:T(8,128)} %inn_hbm.1, f32[16,64,64]{2,1,0:T(8,128)} %ow_hbm.1, ...), custom_call_target="tpu_custom_call" | custom-call | tf_op jit(solution)/shard_map/gradient/pallas_call | solution.py:559
  191.5 2.3 %copy.17 = f32[2,16,16,512]{3,2,1,0:T(8,128)} copy(f32[2,16,16,512]{3,2,1,0:T(8,128)} %gradient.1) | data formatting | bytes 2097152

commit v7 on v5

--- a/solution.py
+++ b/solution.py
@@ -578,7 +578,7 @@
             pltpu.SemaphoreType.REGULAR,
         ],
         compiler_params=pltpu.CompilerParams(
-            collective_id=0, has_side_effects=True, vmem_limit_bytes=56 << 20
+            collective_id=0, has_side_effects=True, vmem_limit_bytes=46 << 20
         ),
         name="gradient",
     )(controls, members, *small, *consts)

time: 192 us -> 204 us (1.062)
  the two profiles are of different devices: /device:TPU:96 before, /device:TPU:100 now
where the time goes in v7:
time: 204 us; the launch traced here: 203 us
  Pallas kernels  189 us (93%)
  local copies, waits for them, and re-layouts  14.7 us (7%)
    pallas_call x1, Pallas kernels, body(): pl.pallas_call(kernel, out_shape=jax.ShapeDtypeStruct(controls.shape, F32...  189 us
    unnamed x29, local copies, waits for them, and re-layouts  14.7 us

profile of v7, /device:TPU:100, one launch (start us, length us, event | category | flops | bytes accessed | tf_op | source)
XLA Modules:
  0.0 203.4 jit_solution(8585368482121510809)
XLA Ops:
  0.0 1.3 copy-done
  1.3 0.0 copy-start.1
  1.3 1.2 copy-done.1
  2.5 0.0 copy-start.2
  2.5 1.2 copy-done.2
  3.7 0.0 copy-start.3
  3.7 1.2 copy-done.3
  4.9 0.0 copy-start.4
  4.9 1.0 copy-done.4
  6.0 0.0 copy-start.5
  6.0 1.0 copy-done.5
  7.0 0.0 copy-start.6
  7.0 0.9 copy-done.6
  8.0 0.0 copy-start.7
  8.0 0.9 copy-done.7
  8.9 0.0 copy-start.8
  8.9 0.9 copy-done.8
  9.9 0.9 copy-done.9
  10.8 0.8 copy-done.10
  11.6 0.8 copy-done.11
  12.4 0.7 copy-done.12
  13.1 0.7 copy-done.13
  13.8 188.7 %gradient.1 = f32[2,16,16,512]{3,2,1,0:T(8,128)S(1)} custom-call(f32[2,16,16,512]{3,2,1,0:T(8,128)S(1)} %copy-done.1, f32[2,16,16,512]{3,2,1,0:T(8,128)S(1)} %copy-done.2, f32[512,512]{1,0:T(8,128)S(1)} %copy-done.3, f32[256,256]{1,0:T(8,128)S(1)} %copy-done.6, f32[5,64,64]{2,1,0:T(8,128)S(1)} %copy-done.9, f32[16,64,64]{2,1,0:T(8,128)S(1)} %copy-done.4, ...), custom_call_target="tpu_custom_call" | custom-call | tf_op jit(solution)/shard_map/gradient/pallas_call | solution.py:541
  202.5 1.0 copy.17
  (6 shorter events, 0.0 us)
Async XLA Ops:
  0.0 1.3 copy-start
  1.3 1.2 copy-start.1
  2.5 1.2 copy-start.2
  3.7 1.2 copy-start.3
  4.9 1.0 copy-start.4
  6.0 1.0 copy-start.5
  7.0 0.9 copy-start.6
  8.0 0.9 copy-start.7
  8.9 0.9 copy-start.8
  9.9 0.9 copy-start.9
  10.8 0.8 copy-start.10
  11.6 0.8 copy-start.11
  12.4 0.7 copy-start.12
  13.1 0.7 copy-start.13
